TPU v7x, 32 devices: a whole 2x2x4 slice. The times are simulated.
32 devices in a mesh: dom: 2 (over y), slab: 4 (over z), shift: 4 (over x, core).
Axes of the slice: x: 2, y: 2, z: 4, core: 2. Of those that a mesh axis runs over, the one named last changes fastest.
Arguments:
- subspace: float32 [16, 64, 512], P(None, ('dom', 'slab')), parts along dimension 1, may hold values from -6 to 6
- potential: float32 [64, 512], P(('dom', 'slab')), parts along dimension 0, may hold values from -2 to 2
- slow_shifts: int32 [4], P('dom'), parts along dimension 0, may hold values from 0 to 7, as said below
Outputs:
- filtered: float32 [16, 64, 512], P('shift', ('dom', 'slab')), parts along dimension 1
There are 2 independent parts, one for each index of `dom`. A program takes and returns all parts, laid end to end along the dimension named above; each array names one. Nothing has to cross between parts.
Inputs may be any that keep to these rules, and one draw needn't show every extreme that they name: `slow_shifts`: two different shift numbers.
All inputs are finite; a program needn't handle non-finite values.
Results may differ from a plain program's by a relative error of at most 0.0003.
Values sent between devices are 32-bit elements; how exact they have to be, the bound alone decides.
A program may use at most 64 MiB of HBM per device.

v0:
```python
import math

import jax
import jax.numpy as jnp
from jax import lax
from jax.sharding import PartitionSpec as P

NS = 8
BLOCK = 8
FAST = 2
SLOW = 4
LY = 32


RADIUS = 4.0


def extended(block, sides, width):
    for axis, dim in sides:
        count = lax.axis_size(axis)
        forward = [(i, i + 1) for i in range(count - 1)]
        backward = [(target, source) for source, target in forward]
        low = lax.ppermute(
            lax.slice_in_dim(block, block.shape[dim] - width, None, axis=dim), axis, forward
        )
        high = lax.ppermute(lax.slice_in_dim(block, 0, width, axis=dim), axis, backward)
        block = jnp.concatenate([low, block, high], axis=dim)
    return block


def plane_sum(values_in):
    width = values_in.shape[-1]
    leading = values_in.shape[:-1]
    rows_zero = jnp.zeros(leading + (LY,), jnp.float32)
    one_zero = jnp.zeros(leading + (1,), jnp.float32)
    column = jnp.arange(width) % LY
    keep_next = (column != LY - 1).astype(jnp.float32)
    keep_prior = (column != 0).astype(jnp.float32)
    running = jnp.concatenate([values_in[..., LY:], rows_zero], -1) + jnp.concatenate(
        [rows_zero, values_in[..., :-LY]], -1
    )
    running = running + jnp.concatenate([values_in[..., 1:], one_zero], -1) * keep_next
    running = running + jnp.concatenate([one_zero, values_in[..., :-1]], -1) * keep_prior
    return running


def combine(vector, neighbours, z_real, z_imag, potential):
    shift_re = z_real[:, None, None, None]
    shift_im = z_imag[:, None, None, None]
    real_part = vector[:, 0]
    imag_part = vector[:, 1]
    out_re = shift_re * real_part - shift_im * imag_part + neighbours[:, 0] - potential * real_part
    out_im = shift_re * imag_part + shift_im * real_part + neighbours[:, 1] - potential * imag_part
    return jnp.stack([out_re, out_im], 1)


def shifted_apply(vector, z_real, z_imag, potential):
    padded = extended(vector, (("slab", 3),), 1)
    neighbours = padded[:, :, :, 2:, :] + padded[:, :, :, :-2, :] + plane_sum(vector)
    return combine(vector, neighbours, z_real, z_imag, potential)


def cscale(num_re, num_im, vector):
    scale_re = num_re[:, :, None, None]
    scale_im = num_im[:, :, None, None]
    return jnp.stack(
        [
            scale_re * vector[:, 0] - scale_im * vector[:, 1],
            scale_re * vector[:, 1] + scale_im * vector[:, 0],
        ],
        1,
    )


def cdiv(top_re, top_im, low_re, low_im):
    magnitude = low_re * low_re + low_im * low_im
    return (
        (top_re * low_re + top_im * low_im) / magnitude,
        (top_im * low_re - top_re * low_im) / magnitude,
    )


def cmul(left_re, left_im, right_re, right_im):
    return (left_re * right_re - left_im * right_im, left_re * right_im + left_im * right_re)


def project(source, vector):
    return (
        jnp.sum(source * vector[:, 0], axis=(2, 3)),
        jnp.sum(source * vector[:, 1], axis=(2, 3)),
    )


def inner(left_vec, right_vec):
    real_sum = jnp.sum(
        left_vec[:, 0] * right_vec[:, 0] + left_vec[:, 1] * right_vec[:, 1], axis=(2, 3)
    )
    imag_sum = jnp.sum(
        left_vec[:, 0] * right_vec[:, 1] - left_vec[:, 1] * right_vec[:, 0], axis=(2, 3)
    )
    return (real_sum, imag_sum)


def step_once(carried, source, z_real, z_imag, potential, active):
    solution, residual, search, rho_re, rho_im = carried
    image = shifted_apply(search, z_real, z_imag, potential)
    den_re, den_im = lax.psum(project(source, image), "slab")
    alpha_re, alpha_im = cdiv(rho_re, rho_im, den_re, den_im)
    middle = residual - cscale(alpha_re, alpha_im, image)
    second = shifted_apply(middle, z_real, z_imag, potential)
    ts_re, ts_im = inner(second, middle)
    t_norm = jnp.sum(second * second, axis=(1, 3, 4))
    ts_re, ts_im, t_norm = lax.psum((ts_re, ts_im, t_norm), "slab")
    omega_re = ts_re / t_norm
    omega_im = ts_im / t_norm
    new_solution = (
        solution + cscale(alpha_re, alpha_im, search) + cscale(omega_re, omega_im, middle)
    )
    new_residual = middle - cscale(omega_re, omega_im, second)
    new_rho_re, new_rho_im = lax.psum(project(source, new_residual), "slab")
    ratio_re, ratio_im = cdiv(new_rho_re, new_rho_im, rho_re, rho_im)
    quot_re, quot_im = cdiv(alpha_re, alpha_im, omega_re, omega_im)
    beta_re, beta_im = cmul(ratio_re, ratio_im, quot_re, quot_im)
    new_search = new_residual + cscale(beta_re, beta_im, search - cscale(omega_re, omega_im, image))
    if active is None:
        return (new_solution, new_residual, new_search, new_rho_re, new_rho_im)
    keep_vec = active[:, None, None, None, None]
    keep_sca = active[:, None]
    return (
        jnp.where(keep_vec, new_solution, solution),
        jnp.where(keep_vec, new_residual, residual),
        jnp.where(keep_vec, new_search, search),
        jnp.where(keep_sca, new_rho_re, rho_re),
        jnp.where(keep_sca, new_rho_im, rho_im),
    )


def repeated(count, state, source, z_real, z_imag, potential, active):

    def advance(step_no, current):
        return step_once(current, source, z_real, z_imag, potential, active)

    return lax.fori_loop(0, count, advance, state)


def shift_values(shift_ids):
    angles = (shift_ids.astype(jnp.float32) + 0.5) * (math.pi / NS)
    return (RADIUS * jnp.cos(angles), RADIUS * jnp.sin(angles))


def weighted(solution, z_real, z_imag):
    weight_re = (z_real / NS)[:, None, None, None]
    weight_im = (z_imag / NS)[:, None, None, None]
    return weight_re * solution[:, 0] - weight_im * solution[:, 1]


def local(subspace, potential, slow_shifts):
    group_count = lax.axis_size("shift")
    my_group = lax.axis_index("shift")
    per_group = NS // group_count
    block_count = subspace.shape[0] // BLOCK
    planes_dev = subspace.shape[1]
    plane_cells = subspace.shape[2]
    rhs_blocks = subspace.reshape(block_count, BLOCK, planes_dev, plane_cells)
    item_count = per_group * block_count
    local_shift = my_group * per_group + jnp.arange(item_count, dtype=jnp.int32) // block_count
    z_real, z_imag = shift_values(local_shift)
    first_slow = jnp.minimum(slow_shifts[0], slow_shifts[1])
    second_slow = jnp.maximum(slow_shifts[0], slow_shifts[1])
    source = jnp.broadcast_to(rhs_blocks[None], (per_group,) + rhs_blocks.shape).reshape(
        item_count, BLOCK, planes_dev, plane_cells
    )
    residual = jnp.stack([source, jnp.zeros_like(source)], 1)
    rho_start = lax.psum(jnp.sum(source * source, axis=(2, 3)), "slab")
    carried = (jnp.zeros_like(residual), residual, residual, rho_start, jnp.zeros_like(rho_start))
    carried = repeated(FAST, carried, source, z_real, z_imag, potential, None)
    kinds = min(2, per_group)
    pick_ids = jnp.arange(kinds * block_count, dtype=jnp.int32)
    pick_shift = jnp.where(pick_ids // block_count == 0, first_slow, second_slow)
    pick_valid = pick_shift // per_group == my_group
    pick_item = pick_shift % per_group * block_count + pick_ids % block_count
    picked = tuple((jnp.take(state_piece, pick_item, axis=0) for state_piece in carried))
    picked_re, picked_im = shift_values(pick_shift)
    picked_source = jnp.take(source, pick_item, axis=0)
    picked = repeated(
        SLOW - FAST, picked, picked_source, picked_re, picked_im, potential, pick_valid
    )
    target = jnp.where(pick_valid, pick_item, item_count)
    carried = tuple(
        (
            whole_state.at[target].set(state_piece, mode="drop")
            for whole_state, state_piece in zip(carried, picked)
        )
    )
    partial_value = jnp.sum(
        weighted(carried[0], z_real, z_imag).reshape(
            per_group, block_count, BLOCK, planes_dev, plane_cells
        ),
        0,
    )
    partial_value = partial_value.reshape(block_count * BLOCK, planes_dev, plane_cells)
    whole = lax.psum(partial_value, "shift")
    slice_width = partial_value.shape[0] // group_count
    return lax.dynamic_slice_in_dim(whole, my_group * slice_width, slice_width, 0)


def solution(mesh):
    return jax.shard_map(
        local,
        mesh=mesh,
        in_specs=(P(None, ("dom", "slab"), None), P(("dom", "slab"), None), P("dom")),
        out_specs=P("shift", ("dom", "slab"), None),
        check_vma=False,
    )
```

profile of v0, /device:TPU:0, one launch (start us, length us, event | category | flops | bytes accessed | tf_op | source)
XLA Modules:
  0.0 372.6 jit_solution(1805108054063914335)
XLA Ops:
  14.5 14.0 %psum.154 = f32[4,8]{1,0:T(4,128)} all-reduce(f32[4,8]{1,0:T(4,128)S(1)} %bitcast.490), channel_id=1, replica_groups=mesh['dom'=2,'slab'=4,'shift'=4] {'slab'}, use_global_device_ids=true, to_apply=%region_1.2 | all-reduce | flops 32 | bytes 256 | tf_op jit(solution)/shard_map/psum | solution.py:174
  29.8 144.3 %while.46 = (s32[]{:T(128)}, f32[4,2,8,8,512]{4,3,2,1,0:T(8,128)}, f32[4,2,8,8,512]{4,3,2,1,0:T(8,128)S(1)}, f32[4,2,8,8,512]{4,3,2,1,0:T(8,128)S(1)}, f32[4,8]{...) while((s32[]{:T(128)}, f32[4,2,8,8,512]{4,3,2,1,0:T(8,128)}, ...), condition=%wide.region_17.18_spmd.clone.clone.clone, body=%wide.region_2.17_spmd.clone.clone.clone.sunk | while | flops 23599452 | bytes 128944552 | solution.py:143
  38.8 3.0 fusion.242
  42.9 9.9 %all-reduce.32 = (f32[4,8]{1,0:T(4,128)S(1)}, f32[4,8]{1,0:T(4,128)S(1)}) all-reduce(f32[4,8]{1,0:T(4,128)S(1)} %get-tuple-element.945, f32[4,8]{1,0:T(4,128)S(1)} %get-tuple-element.946), channel_id=1, replica_groups=mesh['dom'=2,'slab'=4,'shift'=4] {'slab'}, use_global_device_ids=true, to_apply=%region_6.6 | all-reduce | flops 64 | bytes 512 | tf_op jit(solution)/shard_map/while/body/eval_jaxpr/psum | solution.py:107
  62.4 4.4 %collective-permute-done.7 = f32[4,2,8,1,512]{4,3,2,0,1:T(1,128)S(1)} collective-permute-done((f32[4,2,8,1,512]{4,3,2,0,1:T(1,128)S(1)}, f32[4,2,8,1,512]{4,3,2,0,1:T(1,128)S(1)}, u32[]{:S(2)}, u32[]{:S(2)}) %collective-permute-start.7) | collective-permute-done | bytes 131104 | tf_op jit(solution)/shard_map/while/body/eval_jaxpr/ppermute | solution.py:26
  69.7 8.5 %all-reduce.33 = (f32[4,8]{1,0:T(4,128)S(1)}, f32[4,8]{1,0:T(4,128)S(1)}, f32[4,8]{1,0:T(4,128)S(1)}) all-reduce(f32[4,8]{1,0:T(4,128)S(1)} %get-tuple-element.962, f32[4,8]{1,0:T(4,128)S(1)} %fusion.252, f32[4,8]{1,0:T(4,128)S(1)} %get-tuple-element.965), channel_id=1, replica_groups=mesh['dom'=2,'slab'=4,'shift'=4] {'slab'}, use_global_device_ids=true, to_apply=%region_12.12 | all-reduce | flops 96 | bytes 768 | tf_op jit(solution)/shard_map/while/body/eval_jaxpr/psum | solution.py:113
  78.3 2.8 fusion.256
  83.5 10.4 %all-reduce.34 = (f32[4,8]{1,0:T(4,128)S(1)}, f32[4,8]{1,0:T(4,128)S(1)}) all-reduce(f32[4,8]{1,0:T(4,128)S(1)} %get-tuple-element.977, f32[4,8]{1,0:T(4,128)S(1)} %get-tuple-element.978), channel_id=1, replica_groups=mesh['dom'=2,'slab'=4,'shift'=4] {'slab'}, use_global_device_ids=true, to_apply=%region_14.14 | all-reduce | flops 64 | bytes 512 | tf_op jit(solution)/shard_map/while/body/eval_jaxpr/psum | solution.py:120
  111.2 3.0 fusion.242
  115.3 9.6 %all-reduce.32 = (f32[4,8]{1,0:T(4,128)S(1)}, f32[4,8]{1,0:T(4,128)S(1)}) all-reduce(f32[4,8]{1,0:T(4,128)S(1)} %get-tuple-element.945, f32[4,8]{1,0:T(4,128)S(1)} %get-tuple-element.946), channel_id=1, replica_groups=mesh['dom'=2,'slab'=4,'shift'=4] {'slab'}, use_global_device_ids=true, to_apply=%region_6.6 | all-reduce | flops 64 | bytes 512 | tf_op jit(solution)/shard_map/while/body/eval_jaxpr/psum | solution.py:107
  129.7 2.6 collective-permute-start.6
  134.9 4.3 %collective-permute-done.7 = f32[4,2,8,1,512]{4,3,2,0,1:T(1,128)S(1)} collective-permute-done((f32[4,2,8,1,512]{4,3,2,0,1:T(1,128)S(1)}, f32[4,2,8,1,512]{4,3,2,0,1:T(1,128)S(1)}, u32[]{:S(2)}, u32[]{:S(2)}) %collective-permute-start.7) | collective-permute-done | bytes 131104 | tf_op jit(solution)/shard_map/while/body/eval_jaxpr/ppermute | solution.py:26
  142.2 8.5 %all-reduce.33 = (f32[4,8]{1,0:T(4,128)S(1)}, f32[4,8]{1,0:T(4,128)S(1)}, f32[4,8]{1,0:T(4,128)S(1)}) all-reduce(f32[4,8]{1,0:T(4,128)S(1)} %get-tuple-element.962, f32[4,8]{1,0:T(4,128)S(1)} %fusion.252, f32[4,8]{1,0:T(4,128)S(1)} %get-tuple-element.965), channel_id=1, replica_groups=mesh['dom'=2,'slab'=4,'shift'=4] {'slab'}, use_global_device_ids=true, to_apply=%region_12.12 | all-reduce | flops 96 | bytes 768 | tf_op jit(solution)/shard_map/while/body/eval_jaxpr/psum | solution.py:113
  150.7 2.8 fusion.256
  156.0 10.4 %all-reduce.34 = (f32[4,8]{1,0:T(4,128)S(1)}, f32[4,8]{1,0:T(4,128)S(1)}) all-reduce(f32[4,8]{1,0:T(4,128)S(1)} %get-tuple-element.977, f32[4,8]{1,0:T(4,128)S(1)} %get-tuple-element.978), channel_id=1, replica_groups=mesh['dom'=2,'slab'=4,'shift'=4] {'slab'}, use_global_device_ids=true, to_apply=%region_14.14 | all-reduce | flops 64 | bytes 512 | tf_op jit(solution)/shard_map/while/body/eval_jaxpr/psum | solution.py:120
  179.9 2.7 broadcast_select_fusion.2
  187.3 140.7 %while.45 = (s32[]{:T(128)}, f32[4,2,8,8,512]{4,3,2,1,0:T(8,128)}, f32[4,2,8,8,512]{4,3,2,0,1:T(8,128)S(1)}, f32[4,2,8,8,512]{4,3,2,1,0:T(8,128)S(1)}, f32[4,8]{...) while((s32[]{:T(128)}, f32[4,2,8,8,512]{4,3,2,1,0:T(8,128)}, ...), condition=%wide.region_33.36_spmd.clone.clone, body=%wide.region_18.35_spmd.clone.clone.sunk | while | flops 24648196 | bytes 131042208 | solution.py:143
  197.1 2.7 fusion.218
  200.9 11.1 %all-reduce.29 = (f32[4,8]{1,0:T(4,128)S(1)}, f32[4,8]{1,0:T(4,128)S(1)}) all-reduce(f32[4,8]{1,0:T(4,128)S(1)} %get-tuple-element.877, f32[4,8]{1,0:T(4,128)S(1)} %get-tuple-element.878), channel_id=1, replica_groups=mesh['dom'=2,'slab'=4,'shift'=4] {'slab'}, use_global_device_ids=true, to_apply=%region_22.24 | all-reduce | flops 64 | bytes 512 | tf_op jit(solution)/shard_map/while/body/eval_jaxpr/psum | solution.py:107
  220.9 4.4 %collective-permute-done.3 = f32[4,2,8,1,512]{4,3,2,0,1:T(1,128)S(1)} collective-permute-done((f32[4,2,8,1,512]{4,3,2,0,1:T(1,128)S(1)}, f32[4,2,8,1,512]{4,3,2,0,1:T(1,128)S(1)}, u32[]{:S(2)}, u32[]{:S(2)}) %collective-permute-start.3) | collective-permute-done | bytes 131104 | tf_op jit(solution)/shard_map/while/body/eval_jaxpr/ppermute | solution.py:26
  228.5 9.3 %all-reduce.30 = (f32[4,8]{1,0:T(4,128)S(1)}, f32[4,8]{1,0:T(4,128)S(1)}, f32[4,8]{1,0:T(4,128)S(1)}) all-reduce(f32[4,8]{1,0:T(4,128)S(1)} %get-tuple-element.892, f32[4,8]{1,0:T(4,128)S(1)} %fusion.228, f32[4,8]{1,0:T(4,128)S(1)} %get-tuple-element.895), channel_id=1, replica_groups=mesh['dom'=2,'slab'=4,'shift'=4] {'slab'}, use_global_device_ids=true, to_apply=%region_28.30 | all-reduce | flops 96 | bytes 768 | tf_op jit(solution)/shard_map/while/body/eval_jaxpr/psum | solution.py:113
  237.8 3.4 multiply_subtract_fusion.16
  243.3 9.7 %all-reduce.31 = (f32[4,8]{1,0:T(4,128)S(1)}, f32[4,8]{1,0:T(4,128)S(1)}) all-reduce(f32[4,8]{1,0:T(4,128)S(1)} %get-tuple-element.906, f32[4,8]{1,0:T(4,128)S(1)} %get-tuple-element.907), channel_id=1, replica_groups=mesh['dom'=2,'slab'=4,'shift'=4] {'slab'}, use_global_device_ids=true, to_apply=%region_30.32 | all-reduce | flops 64 | bytes 512 | tf_op jit(solution)/shard_map/while/body/eval_jaxpr/psum | solution.py:120
  258.1 2.7 collective-permute-start
  267.9 2.7 fusion.218
  271.7 11.1 %all-reduce.29 = (f32[4,8]{1,0:T(4,128)S(1)}, f32[4,8]{1,0:T(4,128)S(1)}) all-reduce(f32[4,8]{1,0:T(4,128)S(1)} %get-tuple-element.877, f32[4,8]{1,0:T(4,128)S(1)} %get-tuple-element.878), channel_id=1, replica_groups=mesh['dom'=2,'slab'=4,'shift'=4] {'slab'}, use_global_device_ids=true, to_apply=%region_22.24 | all-reduce | flops 64 | bytes 512 | tf_op jit(solution)/shard_map/while/body/eval_jaxpr/psum | solution.py:107
  291.6 4.4 %collective-permute-done.3 = f32[4,2,8,1,512]{4,3,2,0,1:T(1,128)S(1)} collective-permute-done((f32[4,2,8,1,512]{4,3,2,0,1:T(1,128)S(1)}, f32[4,2,8,1,512]{4,3,2,0,1:T(1,128)S(1)}, u32[]{:S(2)}, u32[]{:S(2)}) %collective-permute-start.3) | collective-permute-done | bytes 131104 | tf_op jit(solution)/shard_map/while/body/eval_jaxpr/ppermute | solution.py:26
  299.2 9.3 %all-reduce.30 = (f32[4,8]{1,0:T(4,128)S(1)}, f32[4,8]{1,0:T(4,128)S(1)}, f32[4,8]{1,0:T(4,128)S(1)}) all-reduce(f32[4,8]{1,0:T(4,128)S(1)} %get-tuple-element.892, f32[4,8]{1,0:T(4,128)S(1)} %fusion.228, f32[4,8]{1,0:T(4,128)S(1)} %get-tuple-element.895), channel_id=1, replica_groups=mesh['dom'=2,'slab'=4,'shift'=4] {'slab'}, use_global_device_ids=true, to_apply=%region_28.30 | all-reduce | flops 96 | bytes 768 | tf_op jit(solution)/shard_map/while/body/eval_jaxpr/psum | solution.py:113
  308.5 3.4 multiply_subtract_fusion.16
  314.0 9.7 %all-reduce.31 = (f32[4,8]{1,0:T(4,128)S(1)}, f32[4,8]{1,0:T(4,128)S(1)}) all-reduce(f32[4,8]{1,0:T(4,128)S(1)} %get-tuple-element.906, f32[4,8]{1,0:T(4,128)S(1)} %get-tuple-element.907), channel_id=1, replica_groups=mesh['dom'=2,'slab'=4,'shift'=4] {'slab'}, use_global_device_ids=true, to_apply=%region_30.32 | all-reduce | flops 64 | bytes 512 | tf_op jit(solution)/shard_map/while/body/eval_jaxpr/psum | solution.py:120
  328.6 3.0 scatter_fusion
  334.5 29.8 %all-reduce.37.cloned.1.call-done = f32[16,8,512]{2,1,0:T(8,128)} async-done(((f32[16,8,512]{2,1,0:T(8,128)}), f32[16,8,512]{2,1,0:T(8,128)}) %all-reduce.37.cloned.1.call-update) | async-done | bytes 262160 | tf_op jit(solution)/shard_map/psum | solution.py:202
  (430 shorter events, 142.0 us)
Async XLA Ops:
  6.5 6.8 %copy-start.38 = (f32[16,8,512]{2,1,0:T(8,128)S(1)}, f32[16,8,512]{2,1,0:T(8,128)}, u32[]{:S(2)}) copy-start(f32[16,8,512]{2,1,0:T(8,128)} %param.11) | copy-start | bytes 786436
  6.5 357.8 %all-reduce.37.cloned.1.call-start = ((), (), s32[]{:S(2)}) async-start(), calls=%async_computation | async-start | bytes 524288 | tf_op jit(solution)/shard_map/psum | solution.py:202
  14.4 15.4 %copy-start.39 = (f32[8,512]{1,0:T(8,128)S(1)}, f32[8,512]{1,0:T(8,128)}, u32[]{:S(2)}) copy-start(f32[8,512]{1,0:T(8,128)} %param.12) | copy-start | bytes 49156
  29.9 6.7 %collective-permute-start.4 = (f32[4,2,8,1,512]{4,3,2,0,1:T(1,128)S(1)}, f32[4,2,8,1,512]{4,3,2,0,1:T(1,128)S(1)}, u32[]{:S(2)}, u32[]{:S(2)}) collective-permute-start(f32[4,2,8,1,512]{4,3,2,0,1:T(1,128)S(1)} %get-tuple-element.935), channel_id=1, source_target_pairs={{0,4},{4,8},{8,12},{1,5},{5,9},{9,13},{2,6},{6,10},{10,14},{3,7},{... | collective-permute-start | bytes 393224 | tf_op jit(solution)/shard_map/while/body/eval_jaxpr/ppermute | solution.py:23
  31.3 6.9 %collective-permute-start.5 = (f32[4,2,8,1,512]{4,3,2,0,1:T(1,128)S(1)}, f32[4,2,8,1,512]{4,3,2,0,1:T(1,128)S(1)}, u32[]{:S(2)}, u32[]{:S(2)}) collective-permute-start(f32[4,2,8,1,512]{4,3,2,0,1:T(1,128)S(1)} %get-tuple-element.936), channel_id=1, source_target_pairs={{4,0},{8,4},{12,8},{5,1},{9,5},{13,9},{6,2},{10,6},{14,10},{7,3},{... | collective-permute-start | bytes 393224 | tf_op jit(solution)/shard_map/while/body/eval_jaxpr/ppermute | solution.py:26
  57.5 4.9 %collective-permute-start.6 = (f32[4,2,8,1,512]{4,3,2,0,1:T(1,128)S(1)}, f32[4,2,8,1,512]{4,3,2,0,1:T(1,128)S(1)}, u32[]{:S(2)}, u32[]{:S(2)}) collective-permute-start(f32[4,2,8,1,512]{4,3,2,0,1:T(1,128)S(1)} %get-tuple-element.956), channel_id=1, source_target_pairs={{0,4},{4,8},{8,12},{1,5},{5,9},{9,13},{2,6},{6,10},{10,14},{3,7},{... | collective-permute-start | bytes 393224 | tf_op jit(solution)/shard_map/while/body/eval_jaxpr/ppermute | solution.py:23
  59.9 6.9 %collective-permute-start.7 = (f32[4,2,8,1,512]{4,3,2,0,1:T(1,128)S(1)}, f32[4,2,8,1,512]{4,3,2,0,1:T(1,128)S(1)}, u32[]{:S(2)}, u32[]{:S(2)}) collective-permute-start(f32[4,2,8,1,512]{4,3,2,0,1:T(1,128)S(1)} %get-tuple-element.957), channel_id=1, source_target_pairs={{4,0},{8,4},{12,8},{5,1},{9,5},{13,9},{6,2},{10,6},{14,10},{7,3},{... | collective-permute-start | bytes 393224 | tf_op jit(solution)/shard_map/while/body/eval_jaxpr/ppermute | solution.py:26
  78.3 2.9 copy-start.11
  78.3 2.8 copy-start.13
  101.8 7.2 %collective-permute-start.4 = (f32[4,2,8,1,512]{4,3,2,0,1:T(1,128)S(1)}, f32[4,2,8,1,512]{4,3,2,0,1:T(1,128)S(1)}, u32[]{:S(2)}, u32[]{:S(2)}) collective-permute-start(f32[4,2,8,1,512]{4,3,2,0,1:T(1,128)S(1)} %get-tuple-element.935), channel_id=1, source_target_pairs={{0,4},{4,8},{8,12},{1,5},{5,9},{9,13},{2,6},{6,10},{10,14},{3,7},{... | collective-permute-start | bytes 393224 | tf_op jit(solution)/shard_map/while/body/eval_jaxpr/ppermute | solution.py:23
  103.7 6.9 %collective-permute-start.5 = (f32[4,2,8,1,512]{4,3,2,0,1:T(1,128)S(1)}, f32[4,2,8,1,512]{4,3,2,0,1:T(1,128)S(1)}, u32[]{:S(2)}, u32[]{:S(2)}) collective-permute-start(f32[4,2,8,1,512]{4,3,2,0,1:T(1,128)S(1)} %get-tuple-element.936), channel_id=1, source_target_pairs={{4,0},{8,4},{12,8},{5,1},{9,5},{13,9},{6,2},{10,6},{14,10},{7,3},{... | collective-permute-start | bytes 393224 | tf_op jit(solution)/shard_map/while/body/eval_jaxpr/ppermute | solution.py:26
  129.7 5.2 %collective-permute-start.6 = (f32[4,2,8,1,512]{4,3,2,0,1:T(1,128)S(1)}, f32[4,2,8,1,512]{4,3,2,0,1:T(1,128)S(1)}, u32[]{:S(2)}, u32[]{:S(2)}) collective-permute-start(f32[4,2,8,1,512]{4,3,2,0,1:T(1,128)S(1)} %get-tuple-element.956), channel_id=1, source_target_pairs={{0,4},{4,8},{8,12},{1,5},{5,9},{9,13},{2,6},{6,10},{10,14},{3,7},{... | collective-permute-start | bytes 393224 | tf_op jit(solution)/shard_map/while/body/eval_jaxpr/ppermute | solution.py:23
  132.4 6.9 %collective-permute-start.7 = (f32[4,2,8,1,512]{4,3,2,0,1:T(1,128)S(1)}, f32[4,2,8,1,512]{4,3,2,0,1:T(1,128)S(1)}, u32[]{:S(2)}, u32[]{:S(2)}) collective-permute-start(f32[4,2,8,1,512]{4,3,2,0,1:T(1,128)S(1)} %get-tuple-element.957), channel_id=1, source_target_pairs={{4,0},{8,4},{12,8},{5,1},{9,5},{13,9},{6,2},{10,6},{14,10},{7,3},{... | collective-permute-start | bytes 393224 | tf_op jit(solution)/shard_map/while/body/eval_jaxpr/ppermute | solution.py:26
  150.7 2.9 copy-start.11
  150.7 2.8 copy-start.13
  182.6 2.5 copy-start.41
  188.1 8.4 %collective-permute-start = (f32[4,2,8,1,512]{4,3,2,0,1:T(1,128)}, f32[4,2,8,1,512]{4,3,2,0,1:T(1,128)S(1)}, u32[]{:S(2)}, u32[]{:S(2)}) collective-permute-start(f32[4,2,8,1,512]{4,3,2,0,1:T(1,128)} %get-tuple-element.867), channel_id=1, source_target_pairs={{0,4},{4,8},{8,12},{1,5},{5,9},{9,13},{2,6},{6,10},{10,14},{3,7},{... | collective-permute-start | bytes 393224 | tf_op jit(solution)/shard_map/while/body/eval_jaxpr/ppermute | solution.py:23
  190.0 6.9 %collective-permute-start.1 = (f32[4,2,8,1,512]{4,3,2,0,1:T(1,128)S(1)}, f32[4,2,8,1,512]{4,3,2,0,1:T(1,128)S(1)}, u32[]{:S(2)}, u32[]{:S(2)}) collective-permute-start(f32[4,2,8,1,512]{4,3,2,0,1:T(1,128)S(1)} %get-tuple-element.868), channel_id=1, source_target_pairs={{4,0},{8,4},{12,8},{5,1},{9,5},{13,9},{6,2},{10,6},{14,10},{7,3},{... | collective-permute-start | bytes 393224 | tf_op jit(solution)/shard_map/while/body/eval_jaxpr/ppermute | solution.py:26
  192.7 2.8 copy-start.37
  197.1 2.7 copy-start.25
  217.1 3.8 %collective-permute-start.2 = (f32[4,2,8,1,512]{4,3,2,0,1:T(1,128)S(1)}, f32[4,2,8,1,512]{4,3,2,0,1:T(1,128)S(1)}, u32[]{:S(2)}, u32[]{:S(2)}) collective-permute-start(f32[4,2,8,1,512]{4,3,2,0,1:T(1,128)S(1)} %get-tuple-element.886), channel_id=1, source_target_pairs={{0,4},{4,8},{8,12},{1,5},{5,9},{9,13},{2,6},{6,10},{10,14},{3,7},{... | collective-permute-start | bytes 393224 | tf_op jit(solution)/shard_map/while/body/eval_jaxpr/ppermute | solution.py:23
  218.4 6.9 %collective-permute-start.3 = (f32[4,2,8,1,512]{4,3,2,0,1:T(1,128)S(1)}, f32[4,2,8,1,512]{4,3,2,0,1:T(1,128)S(1)}, u32[]{:S(2)}, u32[]{:S(2)}) collective-permute-start(f32[4,2,8,1,512]{4,3,2,0,1:T(1,128)S(1)} %get-tuple-element.887), channel_id=1, source_target_pairs={{4,0},{8,4},{12,8},{5,1},{9,5},{13,9},{6,2},{10,6},{14,10},{7,3},{... | collective-permute-start | bytes 393224 | tf_op jit(solution)/shard_map/while/body/eval_jaxpr/ppermute | solution.py:26
  243.1 10.0 %copy-start.35 = (f32[4,1,8,8,512]{4,3,2,1,0:T(8,128)S(1)}, f32[4,1,8,8,512]{4,3,2,1,0:T(8,128)}, u32[]{:S(2)}) copy-start(f32[4,1,8,8,512]{4,3,2,1,0:T(8,128)} %get-tuple-element.905) | copy-start | bytes 1572868 | tf_op jit(solution)/shard_map/while
  243.1 10.0 %copy-start.36 = (f32[4,1,8,8,512]{4,3,2,1,0:T(8,128)S(1)}, f32[4,1,8,8,512]{4,3,2,1,0:T(8,128)}, u32[]{:S(2)}) copy-start(f32[4,1,8,8,512]{4,3,2,1,0:T(8,128)} %get-tuple-element.904) | copy-start | bytes 1572868 | tf_op jit(solution)/shard_map/while
  258.1 9.2 %collective-permute-start = (f32[4,2,8,1,512]{4,3,2,0,1:T(1,128)}, f32[4,2,8,1,512]{4,3,2,0,1:T(1,128)S(1)}, u32[]{:S(2)}, u32[]{:S(2)}) collective-permute-start(f32[4,2,8,1,512]{4,3,2,0,1:T(1,128)} %get-tuple-element.867), channel_id=1, source_target_pairs={{0,4},{4,8},{8,12},{1,5},{5,9},{9,13},{2,6},{6,10},{10,14},{3,7},{... | collective-permute-start | bytes 393224 | tf_op jit(solution)/shard_map/while/body/eval_jaxpr/ppermute | solution.py:23
  260.8 6.9 %collective-permute-start.1 = (f32[4,2,8,1,512]{4,3,2,0,1:T(1,128)S(1)}, f32[4,2,8,1,512]{4,3,2,0,1:T(1,128)S(1)}, u32[]{:S(2)}, u32[]{:S(2)}) collective-permute-start(f32[4,2,8,1,512]{4,3,2,0,1:T(1,128)S(1)} %get-tuple-element.868), channel_id=1, source_target_pairs={{4,0},{8,4},{12,8},{5,1},{9,5},{13,9},{6,2},{10,6},{14,10},{7,3},{... | collective-permute-start | bytes 393224 | tf_op jit(solution)/shard_map/while/body/eval_jaxpr/ppermute | solution.py:26
  263.4 2.8 copy-start.37
  267.9 2.7 copy-start.25
  287.8 3.8 %collective-permute-start.2 = (f32[4,2,8,1,512]{4,3,2,0,1:T(1,128)S(1)}, f32[4,2,8,1,512]{4,3,2,0,1:T(1,128)S(1)}, u32[]{:S(2)}, u32[]{:S(2)}) collective-permute-start(f32[4,2,8,1,512]{4,3,2,0,1:T(1,128)S(1)} %get-tuple-element.886), channel_id=1, source_target_pairs={{0,4},{4,8},{8,12},{1,5},{5,9},{9,13},{2,6},{6,10},{10,14},{3,7},{... | collective-permute-start | bytes 393224 | tf_op jit(solution)/shard_map/while/body/eval_jaxpr/ppermute | solution.py:23
  289.2 6.9 %collective-permute-start.3 = (f32[4,2,8,1,512]{4,3,2,0,1:T(1,128)S(1)}, f32[4,2,8,1,512]{4,3,2,0,1:T(1,128)S(1)}, u32[]{:S(2)}, u32[]{:S(2)}) collective-permute-start(f32[4,2,8,1,512]{4,3,2,0,1:T(1,128)S(1)} %get-tuple-element.887), channel_id=1, source_target_pairs={{4,0},{8,4},{12,8},{5,1},{9,5},{13,9},{6,2},{10,6},{14,10},{7,3},{... | collective-permute-start | bytes 393224 | tf_op jit(solution)/shard_map/while/body/eval_jaxpr/ppermute | solution.py:26
  313.8 10.0 %copy-start.35 = (f32[4,1,8,8,512]{4,3,2,1,0:T(8,128)S(1)}, f32[4,1,8,8,512]{4,3,2,1,0:T(8,128)}, u32[]{:S(2)}) copy-start(f32[4,1,8,8,512]{4,3,2,1,0:T(8,128)} %get-tuple-element.905) | copy-start | bytes 1572868 | tf_op jit(solution)/shard_map/while
  313.8 10.0 %copy-start.36 = (f32[4,1,8,8,512]{4,3,2,1,0:T(8,128)S(1)}, f32[4,1,8,8,512]{4,3,2,1,0:T(8,128)}, u32[]{:S(2)}) copy-start(f32[4,1,8,8,512]{4,3,2,1,0:T(8,128)} %get-tuple-element.904) | copy-start | bytes 1572868 | tf_op jit(solution)/shard_map/while
  (114 other events, 116.3 us)
Sparse Core Ops, SparseCore 0:
  334.6 29.6 all-reduce.36
where the time goes:
time: 375 us; the launch traced here: 373 us
  blocking collectives  131 us (35%)
  local copies, waits for them, and re-layouts  74 us (20%)
  other arithmetic  70 us (19%)
  waiting for transfers between devices  54.4 us (15%)
  starting transfers between devices  25.7 us (7%)
  between operations  16.2 us (4%)
    psum x4, blocking collectives, step_once(): den_re, den_im = lax.psum(project(source, image), 'slab')  41.6 us
    psum x4, blocking collectives, step_once(): new_rho_re, new_rho_im = lax.psum(project(source, new_residual), 'slab')  40.1 us
    while x244, local copies, waits for them, and re-layouts  36.3 us
    psum x4, blocking collectives, step_once(): ts_re, ts_im, t_norm = lax.psum((ts_re, ts_im, t_norm), 'slab')  35.6 us
    psum x1, waiting for transfers between devices, local(): whole = lax.psum(partial_value, 'shift')  29.8 us
    sub x14, other arithmetic, cscale(): scale_re * vector[:, 0] - scale_im * vector[:, 1]  23.9 us
    ppermute x8, waiting for transfers between devices, extended(): lax.ppermute(lax.slice_in_dim(block, 0, width, axis=dim), axis, backward)  21.2 us
    ppermute x8, starting transfers between devices, extended(): lax.ppermute(lax.slice_in_dim(block, block.shape[dim] - width, None, axis...  15.3 us
  transfers between devices with their start and end apart: 17, of which 13 were waited for; matrix products, arithmetic and copies ran while one was open for 5% of the time, Pallas kernels for 0%

commit v1 on v0

v1 whole, which is shorter than its diff:
```python
import functools
import math

import jax
import jax.numpy as jnp
import numpy as np
from jax import lax
from jax.experimental import pallas as pl
from jax.experimental.pallas import tpu as pltpu
from jax.sharding import PartitionSpec as P

NS = 8
FAST = 2
SLOW = 4
LY = 32
RADIUS = 4.0
SPAN = 8.0
LANES = 128
ROWS = 8
DEGREE = 2 * SLOW
MOMENTS = 2 * DEGREE + 1
MESH = pl.DeviceIdType.MESH


def shift_constants():
    angles = (np.arange(NS, dtype=np.float32) + np.float32(0.5)) * np.float32(math.pi / NS)
    return (np.float32(RADIUS) * np.cos(angles), np.float32(RADIUS) * np.sin(angles))


def by_lane(lane, values):
    picked = jnp.full(lane.shape, float(values[0]), jnp.float32)
    for index in range(1, len(values)):
        picked = jnp.where(lane == index, float(values[index]), picked)
    return picked


def cdiv(top, low):
    magnitude = low[0] * low[0] + low[1] * low[1]
    return (
        (top[0] * low[0] + top[1] * low[1]) / magnitude,
        (top[1] * low[0] - top[0] * low[1]) / magnitude,
    )


def cmul(left, right):
    return (left[0] * right[0] - left[1] * right[1], left[0] * right[1] + left[1] * right[0])


def cadd(left, right):
    return (left[0] + right[0], left[1] + right[1])


def csub(left, right):
    return (left[0] - right[0], left[1] - right[1])


def times_h(poly):
    count = len(poly)
    out = []
    for j in range(count + 1):
        terms = []
        if j >= 1:
            weight = SPAN if j == 1 else SPAN / 2
            terms.append(tuple(weight * part for part in poly[j - 1]))
        if j + 1 < count:
            terms.append(tuple(SPAN / 2 * part for part in poly[j + 1]))
        if not terms:
            terms.append(tuple(jnp.zeros_like(part) for part in poly[0]))
        total = terms[0]
        for term in terms[1:]:
            total = cadd(total, term)
        out.append(total)
    return out


def shifted(poly, z):
    image = times_h(poly)
    return [cadd(image[j], cmul(z, poly[j])) if j < len(poly) else image[j] for j in range(len(image))]


def total_of(terms):
    terms = list(terms)
    while len(terms) > 1:
        terms = [
            terms[i] + terms[i + 1] if i + 1 < len(terms) else terms[i]
            for i in range(0, len(terms), 2)
        ]
    return terms[0]


def project(poly, moments):
    return tuple(total_of(poly[j][part] * moments[j] for j in range(len(poly))) for part in (0, 1))


def gram_times(gram, poly, count):
    return [
        tuple(total_of(gram[i][j] * poly[j][part] for j in range(len(poly))) for part in (0, 1))
        for i in range(count)
    ]


def solve(moments, z, slow):
    gram = [
        [0.5 * (moments[i + j] + moments[abs(i - j)]) for j in range(DEGREE + 1)]
        for i in range(DEGREE + 1)
    ]
    zero = jnp.zeros_like(moments[0])
    one = jnp.ones_like(moments[0])
    solution = [(zero, zero)] * DEGREE
    residual = [(one, zero)]
    search = [(one, zero)]
    rho = (moments[0], zero)
    for step in range(SLOW):
        image = shifted(search, z)
        alpha = cdiv(rho, project(image, moments))
        middle = [
            csub(residual[j], cmul(alpha, image[j])) if j < len(residual)
            else tuple(-part for part in cmul(alpha, image[j]))
            for j in range(len(image))
        ]
        second = shifted(middle, z)
        low = gram_times(gram, middle, len(second))
        high = gram_times(gram, second, len(second))
        pairs = list(zip(second, low, high))
        ts_re = total_of(s[0] * a[0] + s[1] * a[1] for s, a, _ in pairs)
        ts_im = total_of(s[0] * a[1] - s[1] * a[0] for s, a, _ in pairs)
        t_norm = total_of(s[0] * b[0] + s[1] * b[1] for s, _, b in pairs)
        omega = (ts_re / t_norm, ts_im / t_norm)
        for j in range(len(middle)):
            change = cmul(omega, middle[j])
            if j < len(search):
                change = cadd(change, cmul(alpha, search[j]))
            new = cadd(solution[j], change)
            if step >= FAST:
                new = tuple(jnp.where(slow, a, b) for a, b in zip(new, solution[j]))
            solution[j] = new
        if step == SLOW - 1:
            break
        residual = [
            csub(middle[j], cmul(omega, second[j])) if j < len(middle)
            else tuple(-part for part in cmul(omega, second[j]))
            for j in range(len(second))
        ]
        rho_new = project(residual, moments)
        beta = cmul(cdiv(rho_new, rho), cdiv(alpha, omega))
        rho = rho_new
        inner = [
            csub(search[j], cmul(omega, image[j])) if j < len(search)
            else tuple(-part for part in cmul(omega, image[j]))
            for j in range(len(image))
        ]
        search = [
            cadd(residual[j], cmul(beta, inner[j])) if j < len(inner) else residual[j]
            for j in range(len(residual))
        ]
    return solution


def neighbour_sum(groups, lane):
    depth = groups[0].shape[1]
    low = [pltpu.roll(v, LY, 2) for v in groups]
    high = [pltpu.roll(v, LANES - LY, 2) for v in groups]
    zero = jnp.zeros_like(groups[0])
    out = []
    for g, v in enumerate(groups):
        total = jnp.where(lane < LY, low[g - 1] if g else zero, low[g])
        after = high[g + 1] if g + 1 < len(groups) else zero
        total = total + jnp.where(lane >= LANES - LY, after, high[g])
        total = total + jnp.where(lane % LY == 0, 0.0, pltpu.roll(v, 1, 2))
        total = total + jnp.where(lane % LY == LY - 1, 0.0, pltpu.roll(v, LANES - 1, 2))
        total = total + pltpu.roll(v, 1, 1) + pltpu.roll(v, depth - 1, 1)
        out.append(total)
    return out


def kernel(count, sub_ref, pot_ref, slow_ref, out_ref, field, disorder, parts,
           own_sem, send_sem, recv_sem, part_send, part_recv):
    me = lax.axis_index("slab")
    cols, planes, cells = out_ref.shape
    group_count = cells // LANES
    mine = sub_ref.at[pl.ds(lax.axis_index("shift") * cols, cols)]

    own = [
        pltpu.make_async_copy(mine, field.at[1], own_sem.at[0]),
        pltpu.make_async_copy(pot_ref, disorder.at[1], own_sem.at[1]),
    ]
    for copy in own:
        copy.start()

    barrier = pltpu.get_barrier_semaphore()
    for offset in range(1, count):
        pl.semaphore_signal(
            barrier, inc=1, device_id={"slab": lax.rem(me + offset, count)}, device_id_type=MESH
        )
    pl.semaphore_wait(barrier, count - 1)

    def halo(side):
        target = me + 1 if side == 0 else me - 1
        return [
            pltpu.make_async_remote_copy(
                src_ref=source, dst_ref=place, send_sem=send_sem.at[side, which],
                recv_sem=recv_sem.at[side, which], device_id={"slab": target}, device_id_type=MESH,
            )
            for which, (source, place) in enumerate(
                ((mine, field.at[2 * side]), (pot_ref, disorder.at[2 * side]))
            )
        ]

    has_low, has_high = me > 0, me < count - 1

    @pl.when(has_high)
    def _():
        for copy in halo(0):
            copy.start()

    @pl.when(has_low)
    def _():
        for copy in halo(1):
            copy.start()

    @pl.when(jnp.logical_not(has_low))
    def _():
        field[0] = jnp.zeros((cols, planes, cells), jnp.float32)
        disorder[0] = jnp.zeros((planes, cells), jnp.float32)

    @pl.when(jnp.logical_not(has_high))
    def _():
        field[2] = jnp.zeros((cols, planes, cells), jnp.float32)
        disorder[2] = jnp.zeros((planes, cells), jnp.float32)

    for copy in own:
        copy.wait()

    @pl.when(has_low)
    def _():
        for copy in halo(0):
            copy.wait_recv()

    @pl.when(has_high)
    def _():
        for copy in halo(1):
            copy.wait_recv()

    depth = 3 * planes
    lane = lax.broadcasted_iota(jnp.int32, (1, 1, LANES), 2)
    plane = lax.broadcasted_iota(jnp.int32, (1, depth, LANES), 1)
    inside = jnp.where(has_low, 1, 0) * planes, jnp.where(has_high, 2, 1) * planes
    gain = jnp.where(
        (plane >= planes - inside[0]) & (plane < planes + inside[1]), 2.0 / SPAN, 0.0
    )
    spans = [slice(g * LANES, (g + 1) * LANES) for g in range(group_count)]
    potential = [
        jnp.concatenate([disorder[i, :, s] for i in range(3)], 0)[None] * gain for s in spans
    ]
    before = None
    current = [jnp.concatenate([field[i, :, :, s] for i in range(3)], 1) for s in spans]
    basis = [[v[:, planes:2 * planes] for v in current]]
    for step in range(DEGREE):
        image = [
            gain * total - pot * v
            for total, pot, v in zip(neighbour_sum(current, lane), potential, current)
        ]
        if step == 0:
            following = [0.5 * v for v in image]
        else:
            following = [v - old for v, old in zip(image, before)]
        before, current = current, following
        basis.append([v[:, planes:2 * planes] for v in current])

    lane_of = lax.broadcasted_iota(jnp.int32, (ROWS, LANES), 1)
    payload = jnp.zeros((ROWS, LANES), jnp.float32)
    for k in range(MOMENTS):
        left, right = basis[k // 2], basis[(k + 1) // 2]
        product = total_of(a * b for a, b in zip(left, right))
        rows = jnp.sum(product, axis=1)
        if cols < ROWS:
            rows = jnp.concatenate([rows, jnp.ones((ROWS - cols, LANES), jnp.float32)], 0)
        payload = jnp.where(lane_of == k, jnp.sum(rows, axis=1, keepdims=True), payload)
    parts[me] = payload

    def part(offset):
        return pltpu.make_async_remote_copy(
            src_ref=parts.at[me], dst_ref=parts.at[me], send_sem=part_send.at[offset - 1],
            recv_sem=part_recv.at[offset - 1], device_id={"slab": lax.rem(me + offset, count)},
            device_id_type=MESH,
        )

    for offset in range(1, count):
        part(offset).start()

    z_values = shift_constants()
    z = (by_lane(lane_of, z_values[0]), by_lane(lane_of, z_values[1]))
    slow = (lane_of == slow_ref[0]) | (lane_of == slow_ref[1])

    for offset in range(1, count):
        part(offset).wait_recv()
    whole = total_of(parts[index] for index in range(count))
    sums = [jnp.broadcast_to(whole[:, k:k + 1], (ROWS, LANES)) for k in range(MOMENTS)]
    moments = [sums[0], sums[1]]
    for k in range(2, MOMENTS):
        moments.append(2.0 * sums[k] - sums[k % 2])
    solution_of = solve(moments, z, slow)
    weight = (z[0] / NS, z[1] / NS)
    scales = []
    for re_part, im_part in solution_of:
        value = jnp.where(lane_of < NS, weight[0] * re_part - weight[1] * im_part, 0.0)
        scales.append(jnp.sum(value, axis=1, keepdims=True)[:cols].reshape(cols, 1, 1))
    for g, s in enumerate(spans):
        out_ref[:, :, s] = total_of(scale * v[g] for scale, v in zip(scales, basis))

    for offset in range(1, count):
        part(offset).wait_send()

    @pl.when(has_high)
    def _():
        for copy in halo(0):
            copy.wait_send()

    @pl.when(has_low)
    def _():
        for copy in halo(1):
            copy.wait_send()


def local(subspace, potential, slow_shifts):
    columns, planes, cells = subspace.shape
    count = lax.axis_size("slab")
    cols = columns // lax.axis_size("shift")
    links = max(count - 1, 1)
    return pl.pallas_call(
        functools.partial(kernel, count),
        out_shape=jax.ShapeDtypeStruct((cols, planes, cells), jnp.float32),
        in_specs=[
            pl.BlockSpec(memory_space=pl.ANY),
            pl.BlockSpec(memory_space=pl.ANY),
            pl.BlockSpec(memory_space=pltpu.SMEM),
        ],
        out_specs=pl.BlockSpec(memory_space=pltpu.VMEM),
        scratch_shapes=[
            pltpu.VMEM((3, cols, planes, cells), jnp.float32),
            pltpu.VMEM((3, planes, cells), jnp.float32),
            pltpu.VMEM((count, ROWS, LANES), jnp.float32),
            pltpu.SemaphoreType.DMA((2,)),
            pltpu.SemaphoreType.DMA((2, 2)),
            pltpu.SemaphoreType.DMA((2, 2)),
            pltpu.SemaphoreType.DMA((links,)),
            pltpu.SemaphoreType.DMA((links,)),
        ],
        compiler_params=pltpu.CompilerParams(collective_id=0, has_side_effects=True),
    )(subspace, potential, slow_shifts)


def solution(mesh):
    return jax.shard_map(
        local,
        mesh=mesh,
        in_specs=(P(None, ("dom", "slab"), None), P(("dom", "slab"), None), P("dom")),
        out_specs=P("shift", ("dom", "slab"), None),
        check_vma=False,
    )
```

time: 375 us -> 17.1 us (0.05)
  blocking collectives: 131 us -> 0 us
  local copies, waits for them, and re-layouts: 74 us -> 1.47 us
  other arithmetic: 70 us -> 0 us
  waiting for transfers between devices: 54.4 us -> 0 us
  starting transfers between devices: 25.7 us -> 0 us
  between operations: 16.2 us -> 0.01 us
  Pallas kernels: 0 us -> 15.4 us
    psum x13 -> x0, blocking collectives: 131 us -> none  [the longest x4 41.6 us: step_once(): den_re, den_im = lax.psum(project(source, image), 'slab')]
    while x244 -> x0, local copies, waits for them, and re-layouts: 36.3 us -> none
    sub x32 -> x0, other arithmetic: 30.5 us -> none  [the longest x14 23.9 us: cscale(): scale_re * vector[:, 0] - scale_im * vector[:, 1]]
    psum x1 -> x0, waiting for transfers between devices: 29.8 us -> none  [local(): whole = lax.psum(partial_value, 'shift')]
    ppermute x16 -> x0, starting transfers between devices: 25.7 us -> none  [the longest x8 15.3 us: extended(): lax.ppermute(lax.slice_in_dim(block, block.shape[dim] - width, None, axis...]
    ppermute x16 -> x0, waiting for transfers between devices: 24.5 us -> none  [the longest x8 21.2 us: extended(): lax.ppermute(lax.slice_in_dim(block, 0, width, axis=dim), axis, backward)]
    slice x26 -> x0, local copies, waits for them, and re-layouts: 21.4 us -> none  [the longest x8 8.35 us: plane_sum(): values_in[..., LY:]]
    add x20 -> x0, other arithmetic: 16.8 us -> none  [the longest x8 14.5 us: shifted_apply(): padded[:, :, :, 2:, :] + padded[:, :, :, :-2, :] + plane_sum(vector)]
  transfers between devices with their start and end apart: 17 -> 0, of which waited for: 13 -> 0; matrix products, arithmetic and copies ran while one was open for 5% -> 0% of each run, Pallas kernels for 0% -> 0%
where the time goes in v1:
time: 17.1 us; the launch traced here: 16.9 us
  Pallas kernels  15.4 us (90%)
  local copies, waits for them, and re-layouts  1.47 us (9%)
    pallas_call x1, Pallas kernels, local(): pl.pallas_call(functools.partial(kernel, count), out_shape=jax.ShapeDtype...  15.4 us
    unnamed x1, local copies, waits for them, and re-layouts  1.47 us

profile of v1, /device:TPU:0, one launch (start us, length us, event | category | flops | bytes accessed | tf_op | source)
XLA Modules:
  0.0 16.9 jit_solution(14378724200562383650)
XLA Ops:
  0.0 15.4 %shard_map.37 = f32[4,8,512]{2,1,0:T(8,128)} custom-call(f32[16,8,512]{2,1,0:T(8,128)} %sub_ref.1, f32[8,512]{1,0:T(8,128)} %pot_ref.1, s32[2]{0:T(128)} %slow_ref.1), custom_call_target="tpu_custom_call" | custom-call | tf_op jit(solution)/shard_map/pallas_call | solution.py:330
  15.4 1.5 %copy.5 = f32[4,8,512]{2,1,0:T(8,128)} copy(f32[4,8,512]{2,1,0:T(8,128)} %shard_map.37) | data formatting | bytes 131072

commit v2 on v1

v2 whole, which is shorter than its diff:
```python
import functools
import math

import jax
import jax.numpy as jnp
import numpy as np
from jax import lax
from jax.experimental import pallas as pl
from jax.experimental.pallas import tpu as pltpu
from jax.sharding import PartitionSpec as P

NS = 8
FAST = 2
SLOW = 4
LY = 32
RADIUS = 4.0
SCALE = 4.0
LANES = 128
DEGREE = 2 * SLOW
MESH = pl.DeviceIdType.MESH


def shift_constants():
    angles = (np.arange(NS, dtype=np.float32) + np.float32(0.5)) * np.float32(math.pi / NS)
    return (np.float32(RADIUS) * np.cos(angles), np.float32(RADIUS) * np.sin(angles))


def by_lane(lane, values):
    picked = jnp.full(lane.shape, float(values[0]), jnp.float32)
    for index in range(1, len(values)):
        picked = jnp.where(lane == index, float(values[index]), picked)
    return picked


def cdiv(top, low):
    magnitude = low[0] * low[0] + low[1] * low[1]
    return (
        (top[0] * low[0] + top[1] * low[1]) / magnitude,
        (top[1] * low[0] - top[0] * low[1]) / magnitude,
    )


def cmul(left, right):
    return (left[0] * right[0] - left[1] * right[1], left[0] * right[1] + left[1] * right[0])


def cadd(left, right):
    return (left[0] + right[0], left[1] + right[1])


def csub(left, right):
    return (left[0] - right[0], left[1] - right[1])


def total_of(terms):
    terms = list(terms)
    while len(terms) > 1:
        terms = [
            terms[i] + terms[i + 1] if i + 1 < len(terms) else terms[i]
            for i in range(0, len(terms), 2)
        ]
    return terms[0]


def shifted(poly, z, diagonal, upper):
    count = len(poly)
    out = []
    for j in range(count + 1):
        terms = []
        if j < count:
            terms.append(cmul((z[0] + diagonal[j], z[1]), poly[j]))
        if j >= 1:
            terms.append(tuple(SCALE * part for part in poly[j - 1]))
        if j + 1 < count:
            terms.append(tuple(upper[j + 1] * part for part in poly[j + 1]))
        out.append(tuple(total_of(term[part] for term in terms) for part in (0, 1)))
    return out


def minus(left, factor, right):
    out = []
    for j, value in enumerate(right):
        change = cmul(factor, value)
        out.append(csub(left[j], change) if j < len(left) else (-change[0], -change[1]))
    return out


def solve(norms, diagonal, upper, z, slow):
    zero = jnp.zeros_like(z[0])
    one = jnp.ones_like(z[0])
    solution = [(zero, zero)] * DEGREE
    residual = [(one, zero)]
    search = [(one, zero)]
    for step in range(SLOW):
        image = shifted(search, z, diagonal, upper)
        alpha = cdiv(residual[0], image[0])
        middle = minus(residual, alpha, image)
        second = shifted(middle, z, diagonal, upper)
        heavy = [tuple(norms[j] * part for part in second[j]) for j in range(len(second))]
        pairs = list(zip(heavy, middle))
        ts_re = total_of(s[0] * m[0] + s[1] * m[1] for s, m in pairs)
        ts_im = total_of(s[0] * m[1] - s[1] * m[0] for s, m in pairs)
        t_norm = total_of(h[0] * s[0] + h[1] * s[1] for h, s in zip(heavy, second))
        omega = (ts_re / t_norm, ts_im / t_norm)
        for j in range(len(middle)):
            change = cmul(omega, middle[j])
            if j < len(search):
                change = cadd(change, cmul(alpha, search[j]))
            new = cadd(solution[j], change)
            if step >= FAST:
                new = tuple(jnp.where(slow, a, b) for a, b in zip(new, solution[j]))
            solution[j] = new
        if step == SLOW - 1:
            break
        before = residual[0]
        residual = minus(middle, omega, second)
        beta = cmul(cdiv(residual[0], before), cdiv(alpha, omega))
        inner = minus(search, omega, image)
        search = [
            cadd(residual[j], cmul(beta, inner[j])) if j < len(inner) else residual[j]
            for j in range(len(residual))
        ]
    return solution


def neighbour_sum(groups, lane, row):
    depth = groups[0].shape[0]
    low = [pltpu.roll(v, LY, 1) for v in groups]
    high = [pltpu.roll(v, LANES - LY, 1) for v in groups]
    zero = jnp.zeros_like(groups[0])
    out = []
    for g, v in enumerate(groups):
        after = high[g + 1] if g + 1 < len(groups) else zero
        out.append(total_of([
            jnp.where(lane < LY, low[g - 1] if g else zero, low[g]),
            jnp.where(lane >= LANES - LY, after, high[g]),
            jnp.where(lane % LY == 0, 0.0, pltpu.roll(v, 1, 1)),
            jnp.where(lane % LY == LY - 1, 0.0, pltpu.roll(v, LANES - 1, 1)),
            jnp.where(row == 0, 0.0, pltpu.roll(v, 1, 0)),
            jnp.where(row == depth - 1, 0.0, pltpu.roll(v, depth - 1, 0)),
        ]))
    return out


def dot(left, right):
    product = total_of(a * b for a, b in zip(left, right))
    return jnp.sum(jnp.sum(product, axis=0, keepdims=True), axis=1, keepdims=True)


def filtered_column(groups, potential, slow_first, slow_second):
    depth = groups[0].shape[0]
    lane = lax.broadcasted_iota(jnp.int32, (1, LANES), 1)
    field_lane = lax.broadcasted_iota(jnp.int32, (depth, LANES), 1)
    field_row = lax.broadcasted_iota(jnp.int32, (depth, LANES), 0)
    potential = [v * (1.0 / SCALE) for v in potential]
    basis = [groups]
    norms, diagonal, upper = [dot(groups, groups)], [], [None]
    for step in range(DEGREE):
        current = basis[-1]
        norm = norms[-1]
        inverse = jnp.where(norm > 0.0, 1.0 / norm, 0.0)
        image = [
            total * (1.0 / SCALE) - pot * v
            for total, pot, v in zip(neighbour_sum(current, field_lane, field_row), potential, current)
        ]
        if step:
            image = [v - ratio * old for v, old in zip(image, basis[-2])]
        shift = dot(current, image) * inverse
        following = [v - shift * old for v, old in zip(image, current)]
        basis.append(following)
        norms.append(dot(following, following))
        ratio = norms[-1] * inverse
        diagonal.append(SCALE * shift)
        upper.append(SCALE * ratio)
    z_values = shift_constants()
    z = (by_lane(lane, z_values[0]), by_lane(lane, z_values[1]))
    slow = (lane == slow_first) | (lane == slow_second)
    solution_of = solve(norms, diagonal, upper, z, slow)
    weight = (z[0] / NS, z[1] / NS)
    scales = [
        jnp.sum(
            jnp.where(lane < NS, weight[0] * re_part - weight[1] * im_part, 0.0),
            axis=1, keepdims=True,
        )
        for re_part, im_part in solution_of
    ]
    return [
        total_of(scale * v[g] for scale, v in zip(scales, basis)) for g in range(len(groups))
    ]


def kernel(count, cols, sub_ref, pot_ref, slow_ref, out_ref, field, disorder, result,
           own_sem, send_sem, recv_sem, back_send, back_recv):
    me = lax.axis_index("slab")
    planes, cells = pot_ref.shape
    stride = count // cols
    first = lax.axis_index("shift") * cols
    mine = me // stride
    owner = me % stride == 0

    def when_owner(body):
        if stride == 1:
            body()
        else:
            pl.when(owner)(body)

    def outwards(hop):
        column = lax.rem(mine + hop, cols)
        return [
            pltpu.make_async_remote_copy(
                src_ref=source, dst_ref=place.at[me], send_sem=send_sem.at[hop, which],
                recv_sem=recv_sem.at[me, which], device_id={"slab": column * stride},
                device_id_type=MESH,
            )
            for which, (source, place) in enumerate(
                ((sub_ref.at[first + column], field), (pot_ref, disorder))
            )
        ]

    def inwards(offset):
        source = lax.rem(me + offset, count)
        return [
            pltpu.make_async_remote_copy(
                src_ref=place.at[source], dst_ref=place.at[source], send_sem=send_sem.at[0, which],
                recv_sem=recv_sem.at[source, which], device_id={"slab": source},
                device_id_type=MESH,
            )
            for which, place in enumerate((field, disorder))
        ]

    def home(offset):
        target = lax.rem(me + offset, count)
        return pltpu.make_async_remote_copy(
            src_ref=result.at[target], dst_ref=out_ref.at[mine], send_sem=back_send.at[offset],
            recv_sem=back_recv.at[mine], device_id={"slab": target}, device_id_type=MESH,
        )

    def arriving(hop):
        column = lax.rem(mine + hop, cols)
        return pltpu.make_async_remote_copy(
            src_ref=result.at[0], dst_ref=out_ref.at[column], send_sem=back_send.at[0],
            recv_sem=back_recv.at[column], device_id={"slab": column * stride},
            device_id_type=MESH,
        )

    own = [
        pltpu.make_async_copy(sub_ref.at[first + mine], field.at[me], own_sem.at[0]),
        pltpu.make_async_copy(pot_ref, disorder.at[me], own_sem.at[1]),
    ]

    @when_owner
    def _():
        for copy in own:
            copy.start()

    barrier = pltpu.get_barrier_semaphore()
    for offset in range(1, count):
        pl.semaphore_signal(
            barrier, inc=1, device_id={"slab": lax.rem(me + offset, count)}, device_id_type=MESH
        )
    pl.semaphore_wait(barrier, count - 1)

    if stride > 1:
        @pl.when(jnp.logical_not(owner))
        def _():
            for copy in outwards(0):
                copy.start()

    for hop in range(1, cols):
        for copy in outwards(hop):
            copy.start()

    @when_owner
    def _():
        for copy in own:
            copy.wait()
        for offset in range(1, count):
            for copy in inwards(offset):
                copy.wait_recv()
        spans = [slice(g, g + LANES) for g in range(0, cells, LANES)]
        groups = [field[:, :, s].reshape(count * planes, LANES) for s in spans]
        potential = [disorder[:, :, s].reshape(count * planes, LANES) for s in spans]
        answer = filtered_column(groups, potential, slow_ref[0], slow_ref[1])
        for s, value in zip(spans, answer):
            result[:, :, s] = value.reshape(count, planes, LANES)
        keep = pltpu.make_async_copy(result.at[me], out_ref.at[mine], own_sem.at[0])
        keep.start()
        for offset in range(1, count):
            home(offset).start()
        keep.wait()
        for offset in range(1, count):
            home(offset).wait_send()

    if stride > 1:
        @pl.when(jnp.logical_not(owner))
        def _():
            arriving(0).wait_recv()
            for copy in outwards(0):
                copy.wait_send()

    for hop in range(1, cols):
        arriving(hop).wait_recv()
        for copy in outwards(hop):
            copy.wait_send()


def local(subspace, potential, slow_shifts):
    columns, planes, cells = subspace.shape
    count = lax.axis_size("slab")
    cols = columns // lax.axis_size("shift")
    return pl.pallas_call(
        functools.partial(kernel, count, cols),
        out_shape=jax.ShapeDtypeStruct((cols, planes, cells), jnp.float32),
        in_specs=[
            pl.BlockSpec(memory_space=pl.ANY),
            pl.BlockSpec(memory_space=pl.ANY),
            pl.BlockSpec(memory_space=pltpu.SMEM),
        ],
        out_specs=pl.BlockSpec(memory_space=pl.ANY),
        scratch_shapes=[
            pltpu.VMEM((count, planes, cells), jnp.float32),
            pltpu.VMEM((count, planes, cells), jnp.float32),
            pltpu.VMEM((count, planes, cells), jnp.float32),
            pltpu.SemaphoreType.DMA((2,)),
            pltpu.SemaphoreType.DMA((cols, 2)),
            pltpu.SemaphoreType.DMA((count, 2)),
            pltpu.SemaphoreType.DMA((count,)),
            pltpu.SemaphoreType.DMA((cols,)),
        ],
        compiler_params=pltpu.CompilerParams(collective_id=0, has_side_effects=True),
    )(subspace, potential, slow_shifts)


def solution(mesh):
    return jax.shard_map(
        local,
        mesh=mesh,
        in_specs=(P(None, ("dom", "slab"), None), P(("dom", "slab"), None), P("dom")),
        out_specs=P("shift", ("dom", "slab"), None),
        check_vma=False,
    )
```

time: 17.1 us -> 18.6 us (1.088)
  Pallas kernels: 15.4 us -> 16.8 us
    pallas_call x1, Pallas kernels: 15.4 us -> 16.8 us  [local(): pl.pallas_call(functools.partial(kernel, count, cols), out_shape=jax.Shap...]
where the time goes in v2:
time: 18.6 us; the launch traced here: 18.3 us
  Pallas kernels  16.8 us (90%)
  local copies, waits for them, and re-layouts  1.47 us (8%)
    pallas_call x1, Pallas kernels, local(): pl.pallas_call(functools.partial(kernel, count, cols), out_shape=jax.Shap...  16.8 us
    unnamed x1, local copies, waits for them, and re-layouts  1.47 us

profile of v2, /device:TPU:0, one launch (start us, length us, event | category | flops | bytes accessed | tf_op | source)
XLA Modules:
  0.0 18.3 jit_solution(12170379280586966689)
XLA Ops:
  0.0 16.8 %shard_map.37 = f32[4,8,512]{2,1,0:T(8,128)} custom-call(f32[16,8,512]{2,1,0:T(8,128)} %sub_ref.1, f32[8,512]{1,0:T(8,128)} %pot_ref.1, s32[2]{0:T(128)} %slow_ref.1), custom_call_target="tpu_custom_call" | custom-call | tf_op jit(solution)/shard_map/pallas_call | solution.py:311
  16.8 1.5 %copy.5 = f32[4,8,512]{2,1,0:T(8,128)} copy(f32[4,8,512]{2,1,0:T(8,128)} %shard_map.37) | data formatting | bytes 131072

commit v3 on v2

v3 whole, which is shorter than its diff:
```python
import functools
import math

import jax
import jax.numpy as jnp
import numpy as np
from jax import lax
from jax.experimental import pallas as pl
from jax.experimental.pallas import tpu as pltpu
from jax.sharding import PartitionSpec as P

NS = 8
FAST = 2
SLOW = 4
LY = 32
RADIUS = 4.0
SCALE = 4.0
LANES = 128
DEGREE = 2 * SLOW
PIECES = 2
MESH = pl.DeviceIdType.MESH


def shift_constants():
    angles = (np.arange(NS, dtype=np.float32) + np.float32(0.5)) * np.float32(math.pi / NS)
    return (np.float32(RADIUS) * np.cos(angles), np.float32(RADIUS) * np.sin(angles))


def by_lane(lane, values):
    picked = jnp.full(lane.shape, float(values[0]), jnp.float32)
    for index in range(1, len(values)):
        picked = jnp.where(lane == index, float(values[index]), picked)
    return picked


def cdiv(top, low):
    magnitude = low[0] * low[0] + low[1] * low[1]
    return (
        (top[0] * low[0] + top[1] * low[1]) / magnitude,
        (top[1] * low[0] - top[0] * low[1]) / magnitude,
    )


def cmul(left, right):
    return (left[0] * right[0] - left[1] * right[1], left[0] * right[1] + left[1] * right[0])


def cadd(left, right):
    return (left[0] + right[0], left[1] + right[1])


def csub(left, right):
    return (left[0] - right[0], left[1] - right[1])


def total_of(terms):
    terms = list(terms)
    while len(terms) > 1:
        terms = [
            terms[i] + terms[i + 1] if i + 1 < len(terms) else terms[i]
            for i in range(0, len(terms), 2)
        ]
    return terms[0]


def shifted(poly, z, diagonal, upper):
    count = len(poly)
    out = []
    for j in range(count + 1):
        terms = []
        if j < count:
            terms.append(cmul((z[0] + diagonal[j], z[1]), poly[j]))
        if j >= 1:
            terms.append(tuple(SCALE * part for part in poly[j - 1]))
        if j + 1 < count:
            terms.append(tuple(upper[j + 1] * part for part in poly[j + 1]))
        out.append(tuple(total_of(term[part] for term in terms) for part in (0, 1)))
    return out


def minus(left, factor, right):
    out = []
    for j, value in enumerate(right):
        change = cmul(factor, value)
        out.append(csub(left[j], change) if j < len(left) else (-change[0], -change[1]))
    return out


def solve(norms, diagonal, upper, z, slow):
    zero = jnp.zeros_like(z[0])
    one = jnp.ones_like(z[0])
    solution = [(zero, zero)] * DEGREE
    residual = [(one, zero)]
    search = [(one, zero)]
    for step in range(SLOW):
        image = shifted(search, z, diagonal, upper)
        alpha = cdiv(residual[0], image[0])
        middle = minus(residual, alpha, image)
        second = shifted(middle, z, diagonal, upper)
        heavy = [tuple(norms[j] * part for part in second[j]) for j in range(len(second))]
        pairs = list(zip(heavy, middle))
        ts_re = total_of(s[0] * m[0] + s[1] * m[1] for s, m in pairs)
        ts_im = total_of(s[0] * m[1] - s[1] * m[0] for s, m in pairs)
        t_norm = total_of(h[0] * s[0] + h[1] * s[1] for h, s in zip(heavy, second))
        omega = (ts_re / t_norm, ts_im / t_norm)
        for j in range(len(middle)):
            change = cmul(omega, middle[j])
            if j < len(search):
                change = cadd(change, cmul(alpha, search[j]))
            new = cadd(solution[j], change)
            if step >= FAST:
                new = tuple(jnp.where(slow, a, b) for a, b in zip(new, solution[j]))
            solution[j] = new
        if step == SLOW - 1:
            break
        before = residual[0]
        residual = minus(middle, omega, second)
        beta = cmul(cdiv(residual[0], before), cdiv(alpha, omega))
        inner = minus(search, omega, image)
        search = [
            cadd(residual[j], cmul(beta, inner[j])) if j < len(inner) else residual[j]
            for j in range(len(residual))
        ]
    return solution


def neighbour_sum(groups, lane, row):
    depth = groups[0].shape[1]
    low = [pltpu.roll(v, LY, 2) for v in groups]
    high = [pltpu.roll(v, LANES - LY, 2) for v in groups]
    zero = jnp.zeros_like(groups[0])
    out = []
    for g, v in enumerate(groups):
        after = high[g + 1] if g + 1 < len(groups) else zero
        out.append(total_of([
            jnp.where(lane < LY, low[g - 1] if g else zero, low[g]),
            jnp.where(lane >= LANES - LY, after, high[g]),
            jnp.where(lane % LY == 0, 0.0, pltpu.roll(v, 1, 2)),
            jnp.where(lane % LY == LY - 1, 0.0, pltpu.roll(v, LANES - 1, 2)),
            jnp.where(row == 0, 0.0, pltpu.roll(v, 1, 1)),
            jnp.where(row == depth - 1, 0.0, pltpu.roll(v, depth - 1, 1)),
        ]))
    return out


def dot(left, right):
    product = total_of(a * b for a, b in zip(left, right))
    return jnp.sum(jnp.sum(product, axis=1, keepdims=True), axis=2, keepdims=True)


def column_scales(groups, potential, slow_first, slow_second):
    cols, depth = groups[0].shape[:2]
    field_lane = lax.broadcasted_iota(jnp.int32, (1, depth, LANES), 2)
    field_row = lax.broadcasted_iota(jnp.int32, (1, depth, LANES), 1)
    potential = [v[None] * (1.0 / SCALE) for v in potential]
    basis = [groups]
    norms, diagonal, upper = [dot(groups, groups)], [], [None]
    for step in range(DEGREE):
        current = basis[-1]
        norm = norms[-1]
        inverse = jnp.where(norm > 0.0, 1.0 / norm, 0.0)
        image = [
            total * (1.0 / SCALE) - pot * v
            for total, pot, v in zip(neighbour_sum(current, field_lane, field_row), potential, current)
        ]
        if step:
            image = [v - ratio * old for v, old in zip(image, basis[-2])]
        shift = dot(current, image) * inverse
        following = [v - shift * old for v, old in zip(image, current)]
        basis.append(following)
        norms.append(dot(following, following))
        ratio = norms[-1] * inverse
        diagonal.append(SCALE * shift)
        upper.append(SCALE * ratio)
    norms, diagonal, upper = (
        [None if v is None else v.reshape(cols, 1) for v in values]
        for values in (norms, diagonal, upper)
    )
    lane = lax.broadcasted_iota(jnp.int32, (cols, LANES), 1)
    z_values = shift_constants()
    z = (by_lane(lane, z_values[0]), by_lane(lane, z_values[1]))
    slow = (lane == slow_first) | (lane == slow_second)
    solution_of = solve(norms, diagonal, upper, z, slow)
    weight = (z[0] / NS, z[1] / NS)
    scales = [
        jnp.sum(
            jnp.where(lane < NS, weight[0] * re_part - weight[1] * im_part, 0.0),
            axis=1, keepdims=True,
        ).reshape(cols, 1, 1)
        for re_part, im_part in solution_of
    ]
    return basis, scales


def kernel(count, cols, chunk, sub_ref, pot_ref, slow_ref, out_ref, field, disorder, basis_ref,
           own_sem, send_sem, recv_sem):
    me = lax.axis_index("slab")
    planes, cells = pot_ref.shape
    mine = sub_ref.at[pl.ds(lax.axis_index("shift") * cols, cols)]
    has_low, has_high = me > 0, me < count - 1

    own = [
        pltpu.make_async_copy(pot_ref, disorder.at[me], own_sem.at[0]),
        pltpu.make_async_copy(mine, field.at[me], own_sem.at[1]),
    ]
    for copy in own:
        copy.start()

    barrier = pltpu.get_barrier_semaphore()

    @pl.when(has_low)
    def _():
        pl.semaphore_signal(barrier, inc=1, device_id={"slab": me - 1}, device_id_type=MESH)

    @pl.when(has_high)
    def _():
        pl.semaphore_signal(barrier, inc=1, device_id={"slab": me + 1}, device_id_type=MESH)

    pl.semaphore_wait(barrier, jnp.where(has_low, 1, 0) + jnp.where(has_high, 1, 0))

    half = cols // PIECES

    def passing(slab, side, piece, fresh=False):
        if piece == 0:
            place = disorder.at[slab]
            source = pot_ref if fresh else place
        else:
            rows = pl.ds((piece - 1) * half, half)
            place = field.at[slab, rows]
            source = mine.at[rows] if fresh else place
        return pltpu.make_async_remote_copy(
            src_ref=source, dst_ref=place, send_sem=send_sem.at[side, slab, piece],
            recv_sem=recv_sem.at[slab, piece],
            device_id={"slab": me + 1 if side == 0 else me - 1}, device_id_type=MESH,
        )

    pieces = range(PIECES + 1)
    for piece in pieces:
        @pl.when(has_high)
        def _():
            passing(me, 0, piece, True).start()

        @pl.when(has_low)
        def _():
            passing(me, 1, piece, True).start()

    def relay(hop):
        for piece in pieces:
            @pl.when(me >= hop)
            def _():
                passing(me - hop, 0, piece).wait_recv()

                @pl.when(has_high)
                def _():
                    passing(me - hop, 0, piece).start()

            @pl.when(me + hop < count)
            def _():
                passing(me + hop, 1, piece).wait_recv()

                @pl.when(has_low)
                def _():
                    passing(me + hop, 1, piece).start()

    def drain(hop):
        for piece in pieces:
            @pl.when((me >= hop) & has_high)
            def _():
                passing(me - hop, 0, piece).wait_send()

            @pl.when((me + hop < count) & has_low)
            def _():
                passing(me + hop, 1, piece).wait_send()

    def each_hop(first, body):
        if count <= 8:
            for hop in range(first, count):
                body(hop)
        else:
            lax.fori_loop(first, count, lambda hop, none: (body(hop), none)[1], 0)

    each_hop(1, relay)
    for copy in own:
        copy.wait()

    spans = [slice(g, g + LANES) for g in range(0, cells, LANES)]
    potential = [disorder[:, :, s].reshape(count * planes, LANES) for s in spans]

    def columns_from(start):
        rows = pl.ds(start, chunk)
        groups = [
            jnp.stack([field[:, start + c, :, s].reshape(count * planes, LANES) for c in range(chunk)])
            for s in spans
        ]
        basis, scales = column_scales(groups, potential, slow_ref[0], slow_ref[1])
        for j in range(DEGREE):
            for g, s in enumerate(spans):
                basis_ref[j, :, :, :, s] = basis[j][g].reshape(chunk, count, planes, LANES)
        for s in spans:
            out_ref[rows, :, s] = total_of(
                scale * basis_ref[j, :, me, :, s] for j, scale in enumerate(scales)
            )

    if chunk == cols:
        columns_from(0)
    else:
        lax.fori_loop(
            0, cols // chunk, lambda index, none: (columns_from(index * chunk), none)[1], 0
        )

    each_hop(0, drain)


def local(subspace, potential, slow_shifts):
    columns, planes, cells = subspace.shape
    count = lax.axis_size("slab")
    cols = columns // lax.axis_size("shift")
    chunk = cols if count * planes <= 64 else 1
    return pl.pallas_call(
        functools.partial(kernel, count, cols, chunk),
        out_shape=pltpu.VMEM((cols, planes, cells), jnp.float32),
        in_specs=[
            pl.BlockSpec(memory_space=pl.ANY),
            pl.BlockSpec(memory_space=pl.ANY),
            pl.BlockSpec(memory_space=pltpu.SMEM),
        ],
        out_specs=pl.BlockSpec(memory_space=pltpu.VMEM),
        scratch_shapes=[
            pltpu.VMEM((count, cols, planes, cells), jnp.float32),
            pltpu.VMEM((count, planes, cells), jnp.float32),
            pltpu.VMEM((DEGREE, chunk, count, planes, cells), jnp.float32),
            pltpu.SemaphoreType.DMA((2,)),
            pltpu.SemaphoreType.DMA((2, count, PIECES + 1)),
            pltpu.SemaphoreType.DMA((count, PIECES + 1)),
        ],
        compiler_params=pltpu.CompilerParams(
            collective_id=0, has_side_effects=True, vmem_limit_bytes=40 * 1024 * 1024
        ),
    )(subspace, potential, slow_shifts)


def solution(mesh):
    return jax.shard_map(
        local,
        mesh=mesh,
        in_specs=(P(None, ("dom", "slab"), None), P(("dom", "slab"), None), P("dom")),
        out_specs=P("shift", ("dom", "slab"), None),
        check_vma=False,
    )
```

time: 18.6 us -> 21.6 us (1.16)
  Pallas kernels: 16.8 us -> 18.4 us
  local copies, waits for them, and re-layouts: 1.47 us -> 2.95 us
    pallas_call x1, Pallas kernels: 16.8 us -> 18.4 us  [local(): pl.pallas_call(functools.partial(kernel, count, cols, chunk), out_shape=p...]
    unnamed x1 -> x7, local copies, waits for them, and re-layouts: 1.47 us -> 2.95 us
where the time goes in v3:
time: 21.6 us; the launch traced here: 21.4 us
  Pallas kernels  18.4 us (85%)
  local copies, waits for them, and re-layouts  2.95 us (14%)
    pallas_call x1, Pallas kernels, local(): pl.pallas_call(functools.partial(kernel, count, cols, chunk), out_shape=p...  18.4 us
    unnamed x7, local copies, waits for them, and re-layouts  2.95 us

profile of v3, /device:TPU:0, one launch (start us, length us, event | category | flops | bytes accessed | tf_op | source)
XLA Modules:
  0.0 21.4 jit_solution(17783694832116244260)
XLA Ops:
  0.0 0.0 copy-start
  0.0 0.9 %copy-done = f32[16,8,512]{2,1,0:T(8,128)S(1)} copy-done((f32[16,8,512]{2,1,0:T(8,128)S(1)}, f32[16,8,512]{2,1,0:T(8,128)}, u32[]{:S(2)}) %copy-start) | copy-done | bytes 262168
  1.0 0.0 copy-start.1
  1.0 0.7 %copy-done.1 = f32[8,512]{1,0:T(8,128)S(1)} copy-done((f32[8,512]{1,0:T(8,128)S(1)}, f32[8,512]{1,0:T(8,128)}, u32[]{:S(2)}) %copy-start.1) | copy-done | bytes 16408
  1.7 0.0 copy-start.2
  1.7 0.7 %copy-done.2 = s32[2]{0:T(128)S(1)} copy-done((s32[2]{0:T(128)S(1)}, s32[2]{0:T(128)}, u32[]{:S(2)}) %copy-start.2) | copy-done | bytes 32
  2.3 18.4 %shard_map.37 = f32[4,8,512]{2,1,0:T(8,128)S(1)} custom-call(f32[16,8,512]{2,1,0:T(8,128)S(1)} %copy-done, f32[8,512]{1,0:T(8,128)S(1)} %copy-done.1, s32[2]{0:T(128)S(1)} %copy-done.2), custom_call_target="tpu_custom_call" | custom-call | tf_op jit(solution)/shard_map/pallas_call | solution.py:319
  20.7 0.6 %copy.5 = f32[4,8,512]{2,1,0:T(8,128)} copy(f32[4,8,512]{2,1,0:T(8,128)S(1)} %shard_map.37) | data formatting | bytes 131072
Async XLA Ops:
  0.0 0.9 %copy-start = (f32[16,8,512]{2,1,0:T(8,128)S(1)}, f32[16,8,512]{2,1,0:T(8,128)}, u32[]{:S(2)}) copy-start(f32[16,8,512]{2,1,0:T(8,128)} %sub_ref.1) | copy-start | bytes 786436
  1.0 0.7 %copy-start.1 = (f32[8,512]{1,0:T(8,128)S(1)}, f32[8,512]{1,0:T(8,128)}, u32[]{:S(2)}) copy-start(f32[8,512]{1,0:T(8,128)} %pot_ref.1) | copy-start | bytes 49156
  1.7 0.7 %copy-start.2 = (s32[2]{0:T(128)S(1)}, s32[2]{0:T(128)}, u32[]{:S(2)}) copy-start(s32[2]{0:T(128)} %slow_ref.1) | copy-start | bytes 28

commit v4 on v2

--- a/solution.py
+++ b/solution.py
@@ -310,13 +310,13 @@
     cols = columns // lax.axis_size("shift")
     return pl.pallas_call(
         functools.partial(kernel, count, cols),
-        out_shape=jax.ShapeDtypeStruct((cols, planes, cells), jnp.float32),
+        out_shape=pltpu.VMEM((cols, planes, cells), jnp.float32),
         in_specs=[
             pl.BlockSpec(memory_space=pl.ANY),
             pl.BlockSpec(memory_space=pl.ANY),
             pl.BlockSpec(memory_space=pltpu.SMEM),
         ],
-        out_specs=pl.BlockSpec(memory_space=pl.ANY),
+        out_specs=pl.BlockSpec(memory_space=pltpu.VMEM),
         scratch_shapes=[
             pltpu.VMEM((count, planes, cells), jnp.float32),
             pltpu.VMEM((count, planes, cells), jnp.float32),

time: 18.6 us -> 17.6 us (0.946)
  local copies, waits for them, and re-layouts: 1.47 us -> 0.63 us
    unnamed x1, local copies, waits for them, and re-layouts: 1.47 us -> 0.63 us
where the time goes in v4:
time: 17.6 us; the launch traced here: 17.4 us
  Pallas kernels  16.7 us (95%)
  local copies, waits for them, and re-layouts  0.63 us (4%)
    pallas_call x1, Pallas kernels, local(): pl.pallas_call(functools.partial(kernel, count, cols), out_shape=pltpu.VM...  16.7 us
    unnamed x1, local copies, waits for them, and re-layouts  0.63 us

profile of v4, /device:TPU:0, one launch (start us, length us, event | category | flops | bytes accessed | tf_op | source)
XLA Modules:
  0.0 17.4 jit_solution(16383497417301264916)
XLA Ops:
  0.0 16.7 %shard_map.37 = f32[4,8,512]{2,1,0:T(8,128)S(1)} custom-call(f32[16,8,512]{2,1,0:T(8,128)} %sub_ref.1, f32[8,512]{1,0:T(8,128)} %pot_ref.1, s32[2]{0:T(128)} %slow_ref.1), custom_call_target="tpu_custom_call" | custom-call | tf_op jit(solution)/shard_map/pallas_call | solution.py:311
  16.8 0.6 %copy.5 = f32[4,8,512]{2,1,0:T(8,128)} copy(f32[4,8,512]{2,1,0:T(8,128)S(1)} %shard_map.37) | data formatting | bytes 131072

commit v5 on v4

--- a/solution.py
+++ b/solution.py
@@ -163,9 +163,9 @@
             total * (1.0 / SCALE) - pot * v
             for total, pot, v in zip(neighbour_sum(current, field_lane, field_row), potential, current)
         ]
+        shift = dot(current, image) * inverse
         if step:
             image = [v - ratio * old for v, old in zip(image, basis[-2])]
-        shift = dot(current, image) * inverse
         following = [v - shift * old for v, old in zip(image, current)]
         basis.append(following)
         norms.append(dot(following, following))
@@ -190,11 +190,15 @@
 
 
 def kernel(count, cols, sub_ref, pot_ref, slow_ref, out_ref, field, disorder, result,
-           own_sem, send_sem, recv_sem, back_send, back_recv):
+           own_sem, send_sem, recv_sem, back_send, back_recv, pair_sem):
     me = lax.axis_index("slab")
     planes, cells = pot_ref.shape
     stride = count // cols
-    first = lax.axis_index("shift") * cols
+    group = lax.axis_index("shift")
+    first = group * cols
+    half = cells // 2
+    share = pl.ds(pl.multiple_of(lax.rem(group, 2) * half, half), half)
+    partner = {"shift": group + 1 - 2 * lax.rem(group, 2)}
     mine = me // stride
     owner = me % stride == 0
 
@@ -208,25 +212,33 @@
         column = lax.rem(mine + hop, cols)
         return [
             pltpu.make_async_remote_copy(
-                src_ref=source, dst_ref=place.at[me], send_sem=send_sem.at[hop, which],
+                src_ref=source, dst_ref=place, send_sem=send_sem.at[hop, which],
                 recv_sem=recv_sem.at[me, which], device_id={"slab": column * stride},
                 device_id_type=MESH,
             )
             for which, (source, place) in enumerate(
-                ((sub_ref.at[first + column], field), (pot_ref, disorder))
+                (
+                    (pot_ref.at[:, share], disorder.at[me, :, share]),
+                    (sub_ref.at[first + column], field.at[me]),
+                )
             )
         ]
 
-    def inwards(offset):
+    def inwards(offset, which):
         source = lax.rem(me + offset, count)
-        return [
-            pltpu.make_async_remote_copy(
-                src_ref=place.at[source], dst_ref=place.at[source], send_sem=send_sem.at[0, which],
-                recv_sem=recv_sem.at[source, which], device_id={"slab": source},
-                device_id_type=MESH,
-            )
-            for which, place in enumerate((field, disorder))
-        ]
+        place = field.at[source] if which else disorder.at[source, :, share]
+        return pltpu.make_async_remote_copy(
+            src_ref=place, dst_ref=place, send_sem=send_sem.at[0, which],
+            recv_sem=recv_sem.at[source, which], device_id={"slab": source},
+            device_id_type=MESH,
+        )
+
+    def paired(lanes):
+        return pltpu.make_async_remote_copy(
+            src_ref=disorder.at[:, :, lanes], dst_ref=disorder.at[:, :, lanes],
+            send_sem=pair_sem.at[0], recv_sem=pair_sem.at[1], device_id=partner,
+            device_id_type=MESH,
+        )
 
     def home(offset):
         target = lax.rem(me + offset, count)
@@ -245,7 +257,7 @@
 
     own = [
         pltpu.make_async_copy(sub_ref.at[first + mine], field.at[me], own_sem.at[0]),
-        pltpu.make_async_copy(pot_ref, disorder.at[me], own_sem.at[1]),
+        pltpu.make_async_copy(pot_ref.at[:, share], disorder.at[me, :, share], own_sem.at[1]),
     ]
 
     @when_owner
@@ -258,7 +270,8 @@
         pl.semaphore_signal(
             barrier, inc=1, device_id={"slab": lax.rem(me + offset, count)}, device_id_type=MESH
         )
-    pl.semaphore_wait(barrier, count - 1)
+    pl.semaphore_signal(barrier, inc=1, device_id=partner, device_id_type=MESH)
+    pl.semaphore_wait(barrier, count)
 
     if stride > 1:
         @pl.when(jnp.logical_not(owner))
@@ -266,17 +279,21 @@
             for copy in outwards(0):
                 copy.start()
 
-    for hop in range(1, cols):
-        for copy in outwards(hop):
-            copy.start()
+    for which in range(2):
+        for hop in range(1, cols):
+            outwards(hop)[which].start()
 
     @when_owner
     def _():
         for copy in own:
             copy.wait()
         for offset in range(1, count):
-            for copy in inwards(offset):
-                copy.wait_recv()
+            inwards(offset, 0).wait_recv()
+        paired(share).start()
+        for offset in range(1, count):
+            inwards(offset, 1).wait_recv()
+        other = pl.ds(pl.multiple_of(half - lax.rem(group, 2) * half, half), half)
+        paired(other).wait_recv()
         spans = [slice(g, g + LANES) for g in range(0, cells, LANES)]
         groups = [field[:, :, s].reshape(count * planes, LANES) for s in spans]
         potential = [disorder[:, :, s].reshape(count * planes, LANES) for s in spans]
@@ -288,6 +305,7 @@
         for offset in range(1, count):
             home(offset).start()
         keep.wait()
+        paired(share).wait_send()
         for offset in range(1, count):
             home(offset).wait_send()
 
@@ -326,6 +344,7 @@
             pltpu.SemaphoreType.DMA((count, 2)),
             pltpu.SemaphoreType.DMA((count,)),
             pltpu.SemaphoreType.DMA((cols,)),
+            pltpu.SemaphoreType.DMA((2,)),
         ],
         compiler_params=pltpu.CompilerParams(collective_id=0, has_side_effects=True),
     )(subspace, potential, slow_shifts)

time: 17.6 us -> 17.1 us (0.972)
  Pallas kernels: 16.7 us -> 16.3 us
    pallas_call x1, Pallas kernels: 16.7 us -> 16.3 us  [local(): pl.pallas_call(functools.partial(kernel, count, cols), out_shape=pltpu.VM...]
where the time goes in v5:
time: 17.1 us; the launch traced here: 17 us
  Pallas kernels  16.3 us (95%)
  local copies, waits for them, and re-layouts  0.63 us (4%)
    pallas_call x1, Pallas kernels, local(): pl.pallas_call(functools.partial(kernel, count, cols), out_shape=pltpu.VM...  16.3 us
    unnamed x1, local copies, waits for them, and re-layouts  0.63 us

profile of v5, /device:TPU:0, one launch (start us, length us, event | category | flops | bytes accessed | tf_op | source)
XLA Modules:
  0.0 17.0 jit_solution(3691182607174292022)
XLA Ops:
  0.0 16.3 %shard_map.37 = f32[4,8,512]{2,1,0:T(8,128)S(1)} custom-call(f32[16,8,512]{2,1,0:T(8,128)} %sub_ref.1, f32[8,512]{1,0:T(8,128)} %pot_ref.1, s32[2]{0:T(128)} %slow_ref.1), custom_call_target="tpu_custom_call" | custom-call | tf_op jit(solution)/shard_map/pallas_call | solution.py:329
  16.3 0.6 %copy.5 = f32[4,8,512]{2,1,0:T(8,128)} copy(f32[4,8,512]{2,1,0:T(8,128)S(1)} %shard_map.37) | data formatting | bytes 131072

commit v6 on v5

--- a/solution.py
+++ b/solution.py
@@ -190,7 +190,8 @@
 
 
 def kernel(count, cols, sub_ref, pot_ref, slow_ref, out_ref, field, disorder, result,
-           own_sem, send_sem, recv_sem, back_send, back_recv, pair_sem):
+           own_sem, send_sem, recv_sem, back_send, back_recv, pair_sem,
+           staged, staged_pot):
     me = lax.axis_index("slab")
     planes, cells = pot_ref.shape
     stride = count // cols
@@ -218,8 +219,8 @@
             )
             for which, (source, place) in enumerate(
                 (
-                    (pot_ref.at[:, share], disorder.at[me, :, share]),
-                    (sub_ref.at[first + column], field.at[me]),
+                    (staged_pot.at[:, share], disorder.at[me, :, share]),
+                    (staged.at[column], field.at[me]),
                 )
             )
         ]
@@ -260,6 +261,13 @@
         pltpu.make_async_copy(pot_ref.at[:, share], disorder.at[me, :, share], own_sem.at[1]),
     ]
 
+    stage = [
+        pltpu.make_async_copy(sub_ref.at[pl.ds(first, cols)], staged, own_sem.at[2]),
+        pltpu.make_async_copy(pot_ref, staged_pot, own_sem.at[3]),
+    ]
+    for copy in stage:
+        copy.start()
+
     @when_owner
     def _():
         for copy in own:
@@ -271,6 +279,8 @@
             barrier, inc=1, device_id={"slab": lax.rem(me + offset, count)}, device_id_type=MESH
         )
     pl.semaphore_signal(barrier, inc=1, device_id=partner, device_id_type=MESH)
+    for copy in stage:
+        copy.wait()
     pl.semaphore_wait(barrier, count)
 
     if stride > 1:
@@ -339,12 +349,14 @@
             pltpu.VMEM((count, planes, cells), jnp.float32),
             pltpu.VMEM((count, planes, cells), jnp.float32),
             pltpu.VMEM((count, planes, cells), jnp.float32),
-            pltpu.SemaphoreType.DMA((2,)),
+            pltpu.SemaphoreType.DMA((4,)),
             pltpu.SemaphoreType.DMA((cols, 2)),
             pltpu.SemaphoreType.DMA((count, 2)),
             pltpu.SemaphoreType.DMA((count,)),
             pltpu.SemaphoreType.DMA((cols,)),
             pltpu.SemaphoreType.DMA((2,)),
+            pltpu.VMEM((cols, planes, cells), jnp.float32),
+            pltpu.VMEM((planes, cells), jnp.float32),
         ],
         compiler_params=pltpu.CompilerParams(collective_id=0, has_side_effects=True),
     )(subspace, potential, slow_shifts)

time: 17.1 us -> 16.9 us (0.988)
  Pallas kernels: 16.3 us -> 16.1 us
    pallas_call x1, Pallas kernels: 16.3 us -> 16.1 us  [local(): pl.pallas_call(functools.partial(kernel, count, cols), out_shape=pltpu.VM...]
where the time goes in v6:
time: 16.9 us; the launch traced here: 16.8 us
  Pallas kernels  16.1 us (95%)
  local copies, waits for them, and re-layouts  0.63 us (4%)
    pallas_call x1, Pallas kernels, local(): pl.pallas_call(functools.partial(kernel, count, cols), out_shape=pltpu.VM...  16.1 us
    unnamed x1, local copies, waits for them, and re-layouts  0.63 us

profile of v6, /device:TPU:0, one launch (start us, length us, event | category | flops | bytes accessed | tf_op | source)
XLA Modules:
  0.0 16.8 jit_solution(3048848637467389882)
XLA Ops:
  0.0 16.1 %shard_map.37 = f32[4,8,512]{2,1,0:T(8,128)S(1)} custom-call(f32[16,8,512]{2,1,0:T(8,128)} %sub_ref.1, f32[8,512]{1,0:T(8,128)} %pot_ref.1, s32[2]{0:T(128)} %slow_ref.1), custom_call_target="tpu_custom_call" | custom-call | tf_op jit(solution)/shard_map/pallas_call | solution.py:339
  16.1 0.6 %copy.5 = f32[4,8,512]{2,1,0:T(8,128)} copy(f32[4,8,512]{2,1,0:T(8,128)S(1)} %shard_map.37) | data formatting | bytes 131072

commit v7 on v6

--- a/solution.py
+++ b/solution.py
@@ -136,8 +136,8 @@
             jnp.where(lane >= LANES - LY, after, high[g]),
             jnp.where(lane % LY == 0, 0.0, pltpu.roll(v, 1, 1)),
             jnp.where(lane % LY == LY - 1, 0.0, pltpu.roll(v, LANES - 1, 1)),
-            jnp.where(row == 0, 0.0, pltpu.roll(v, 1, 0)),
-            jnp.where(row == depth - 1, 0.0, pltpu.roll(v, depth - 1, 0)),
+            jnp.concatenate([zero[:1], v[:-1]], 0),
+            jnp.concatenate([v[1:], zero[:1]], 0),
         ]))
     return out
 
@@ -290,7 +290,7 @@
                 copy.start()
 
     for which in range(2):
-        for hop in range(1, cols):
+        for hop in sorted(range(1, cols), key=lambda h: abs(2 * h - cols)):
             outwards(hop)[which].start()
 
     @when_owner

time: 16.9 us -> 16.9 us (level)
  no operation moved by 1% of the time
where the time goes in v7:
time: 16.9 us; the launch traced here: 16.8 us
  Pallas kernels  16.1 us (95%)
  local copies, waits for them, and re-layouts  0.63 us (4%)
    pallas_call x1, Pallas kernels, local(): pl.pallas_call(functools.partial(kernel, count, cols), out_shape=pltpu.VM...  16.1 us
    unnamed x1, local copies, waits for them, and re-layouts  0.63 us

profile of v7, /device:TPU:0, one launch (start us, length us, event | category | flops | bytes accessed | tf_op | source)
XLA Modules:
  0.0 16.8 jit_solution(11345627348284782810)
XLA Ops:
  0.0 16.1 %shard_map.37 = f32[4,8,512]{2,1,0:T(8,128)S(1)} custom-call(f32[16,8,512]{2,1,0:T(8,128)} %sub_ref.1, f32[8,512]{1,0:T(8,128)} %pot_ref.1, s32[2]{0:T(128)} %slow_ref.1), custom_call_target="tpu_custom_call" | custom-call | tf_op jit(solution)/shard_map/pallas_call | solution.py:339
  16.1 0.6 %copy.5 = f32[4,8,512]{2,1,0:T(8,128)} copy(f32[4,8,512]{2,1,0:T(8,128)S(1)} %shard_map.37) | data formatting | bytes 131072
